TPU v7x, 32 devices: a whole 2x2x4 slice. The times are simulated.
32 devices in a mesh: groups: 2 (over x), seq: 16 (over z, y, core).
Axes of the slice: x: 2, y: 2, z: 4, core: 2. Of those that a mesh axis runs over, the one named last changes fastest.
Arguments:
- audio_stream: bfloat16 [64, 2048], P(('groups', 'seq')), parts along dimension 0, may hold values from -6 to 6
- audio_qkv: bfloat16 [3, 64, 2048], P(None, ('groups', 'seq')), parts along dimension 1, may hold values from -6 to 6
- video_qkv: bfloat16 [3, 4096, 2048], P(None, ('groups', 'seq')), parts along dimension 1, may hold values from -6 to 6
- attention_out: bfloat16 [2048, 2048], P('seq'), may hold values from -0.125 to 0.125
- norm_gain: float32 [2048], replicated, may hold values from 0.25 to 1.75
- weight_in: bfloat16 [2048, 8192], P(None, 'seq'), may hold values from -0.125 to 0.125
- weight_out: bfloat16 [8192, 2048], P('seq'), may hold values from -0.0625 to 0.0625
Outputs:
- video_mix: bfloat16 [4096, 2048], P(('groups', 'seq')), parts along dimension 0
- audio_result: bfloat16 [64, 2048], P(('groups', 'seq')), parts along dimension 0
There are 2 independent parts, one for each index of `groups`. A program takes and returns all parts, laid end to end along the dimension named above; an argument that names none is the same for every part. Nothing has to cross between parts.
All inputs are finite; a program needn't handle non-finite values.
Results may differ from a plain program's by a relative error of at most 0.008.
Values may be sent and summed in bfloat16 or wider, within the bound.
A program may use at most 128 MiB of HBM per device.

v0:
```python
import math

import jax
import jax.numpy as jnp
from jax import lax
from jax.sharding import PartitionSpec as P

HEADS = 32
HD = 64


epsilon = 1e-06


def joined_2(part, axis, combine):
    gathered = jax.tree.map(lambda a: lax.all_gather(a, axis), part)

    def take(source):
        return jax.tree.map(lambda a: lax.dynamic_index_in_dim(a, source, 0, False), gathered)

    return lax.fori_loop(
        1, lax.axis_size(axis), lambda source, state: combine(state, take(source)), take(0)
    )


def head_view(block):
    return block.reshape(block.shape[0], HEADS, HD)


def scores_of(queries, key_rows):
    logits = jnp.einsum(
        "rhd,shd->rhs", head_view(queries), head_view(key_rows), preferred_element_type=jnp.float32
    )
    return logits * (1.0 / math.sqrt(HD))


def weighted(weights, value_rows):
    return jnp.einsum(
        "rhs,shd->rhd",
        weights.astype(jnp.bfloat16),
        head_view(value_rows),
        preferred_element_type=jnp.float32,
    )


def local(audio_stream, audio_qkv, video_qkv, attention_out, norm_gain, weight_in, weight_out):
    video_rows = video_qkv.shape[1]
    video_queries = video_qkv[0]
    gathered = lax.all_gather(audio_qkv, "seq", axis=1, tiled=True)
    all_queries = gathered[0]
    row_peak = jnp.full((video_rows, HEADS), -jnp.inf, jnp.float32)
    row_total = jnp.zeros((video_rows, HEADS), jnp.float32)
    running = jnp.zeros((video_rows, HEADS, HD), jnp.float32)
    key_rows = gathered[1]
    value_rows = gathered[2]
    logits = scores_of(video_queries, key_rows)
    new_peak = jnp.max(logits, axis=2)
    rescale = jnp.exp(row_peak - new_peak)
    weights = jnp.exp(logits - new_peak[:, :, None])
    row_total = row_total * rescale + jnp.sum(weights, axis=2)
    running = running * rescale[:, :, None] + weighted(weights, value_rows)
    row_peak, row_total, running = (new_peak, row_total, running)
    video_mix = (
        (running / row_total[:, :, None]).reshape(video_rows, HEADS * HD).astype(jnp.bfloat16)
    )
    audio_count = all_queries.shape[0]
    logits = scores_of(all_queries, video_qkv[1])
    local_peak = jnp.max(logits, axis=2)
    weights = jnp.exp(logits - local_peak[:, :, None])
    numerator = weighted(weights, video_qkv[2]).reshape(audio_count, HEADS * HD)
    partial_value = (local_peak, jnp.sum(weights, axis=2), numerator)

    def combine(earlier, later):
        highest = jnp.maximum(earlier[0], later[0])
        left_scale = jnp.exp(earlier[0] - highest)
        right_scale = jnp.exp(later[0] - highest)
        left_sum = head_view(earlier[2]) * left_scale[:, :, None]
        right_sum = head_view(later[2]) * right_scale[:, :, None]
        joined = (left_sum + right_sum).reshape(earlier[2].shape)
        return (highest, earlier[1] * left_scale + later[1] * right_scale, joined)

    merged = joined_2(partial_value, "seq", combine)
    row_total = merged[1]
    attention_all = (
        (head_view(merged[2]) / row_total[:, :, None])
        .reshape(audio_count, HEADS * HD)
        .astype(jnp.bfloat16)
    )
    slab_width = attention_out.shape[0]
    columns = lax.dynamic_slice_in_dim(
        attention_all, lax.axis_index("seq") * slab_width, slab_width, 1
    )
    mixed_audio = audio_stream.astype(jnp.float32) + lax.psum_scatter(
        jnp.dot(columns, attention_out, preferred_element_type=jnp.float32),
        "seq",
        scatter_dimension=0,
        tiled=True,
    )
    mean_square = jnp.mean(mixed_audio * mixed_audio, axis=1, keepdims=True)
    normed = (mixed_audio * lax.rsqrt(mean_square + epsilon) * norm_gain).astype(jnp.bfloat16)
    hidden = jax.nn.gelu(
        jnp.dot(
            lax.all_gather(normed, "seq", axis=0, tiled=True),
            weight_in,
            preferred_element_type=jnp.float32,
        ),
        approximate=True,
    ).astype(jnp.bfloat16)
    audio_result = (
        mixed_audio
        + lax.psum_scatter(
            jnp.dot(hidden, weight_out, preferred_element_type=jnp.float32),
            "seq",
            scatter_dimension=0,
            tiled=True,
        )
    ).astype(jnp.bfloat16)
    return (video_mix, audio_result)


def solution(mesh):
    placed = (
        P(("groups", "seq"), None),
        P(None, ("groups", "seq"), None),
        P(None, ("groups", "seq"), None),
        P("seq", None),
        P(),
        P(None, "seq"),
        P("seq", None),
    )
    return jax.shard_map(
        local,
        mesh=mesh,
        in_specs=placed,
        out_specs=(P(("groups", "seq"), None), P(("groups", "seq"), None)),
        check_vma=False,
    )
```

profile of v0, /device:TPU:0, one launch (start us, length us, event | category | flops | bytes accessed | tf_op | source)
XLA Modules:
  0.0 343.7 jit_solution(9186944096646851286)
XLA Ops:
  7.2 2.4 fusion.45
  9.7 24.6 %all_gather.21 = bf16[3,32,2048]{2,0,1:T(4,128)(2,1)S(1)} all-gather(bf16[3,2,2048]{2,0,1:T(4,128)(2,1)S(1)} %copy.36), channel_id=1, replica_groups=mesh['groups'=2,'seq'=16] {'seq'}, dimensions={1}, use_global_device_ids=true | all-gather | bytes 417792 | tf_op jit(solution)/shard_map/all_gather | solution.py:49
  34.3 2.3 slice_reduce_fusion
  36.6 1.0 copy.40
  37.6 1.2 reshape_squeeze.22
  38.7 0.3 copy.44
  39.0 1.4 fusion.47
  40.4 0.4 convolution_bitcast_fusion.1
  40.9 0.3 copy.45
  41.2 0.9 all_gather_reshape.3
  42.1 0.7 copy.42
  42.8 1.3 copy.37
  44.1 1.2 reshape_squeeze.18
  45.3 0.9 reshape_squeeze.20
  46.3 19.1 %all-gather = f32[512,32]{1,0:T(8,128)S(1)} all-gather(f32[32,32]{1,0:T(8,128)} %copy.42), channel_id=2, replica_groups=mesh['groups'=2,'seq'=16] {'seq'}, dimensions={0}, use_global_device_ids=true | all-gather | bytes 69632 | tf_op jit(solution)/shard_map/all_gather | solution.py:16
  65.4 0.7 copy-done.3
  66.1 0.4 fusion.11
  66.5 21.6 %all-gather.1 = f32[512,32]{1,0:T(8,128)} all-gather(f32[32,32]{1,0:T(8,128)S(1)} %copy.43), channel_id=3, replica_groups=mesh['groups'=2,'seq'=16] {'seq'}, dimensions={0}, use_global_device_ids=true | all-gather | bytes 69632 | tf_op jit(solution)/shard_map/all_gather | solution.py:16
  88.1 0.7 slice.33
  88.8 1.2 dynamic-slice
  90.7 0.3 fusion.46
  91.0 0.8 copy-done.1
  92.0 1.0 slice_bitcast_fusion
  93.0 39.2 %while.19 = (s32[]{:T(128)}, f32[32,32]{1,0:T(8,128)S(1)}, f32[32,32]{1,0:T(8,128)S(1)}, f32[32,2048]{1,0:T(8,128)S(1)}, f32[16,32,32]{2,1,0:T(8,128)}, /*index=...) while((s32[]{:T(128)}, f32[32,32]{1,0:T(8,128)S(1)}, ...), condition=%wide.region_5.6_spmd, body=%wide.region_4.5_spmd.sunk | while | flops 202757 | bytes 2924695 | solution.py:21
  93.0 0.8 fusion.59
  94.6 1.1 fusion.60
  95.6 0.8 fusion.59
  97.2 1.1 fusion.60
  98.3 0.8 fusion.59
  99.8 1.1 fusion.60
  100.9 0.8 fusion.59
  102.4 1.1 fusion.60
  103.5 0.8 fusion.59
  105.0 1.1 fusion.60
  106.1 0.8 fusion.59
  107.6 1.1 fusion.60
  108.7 0.8 fusion.59
  110.2 1.1 fusion.60
  111.3 0.8 fusion.59
  112.9 1.1 fusion.60
  113.9 0.8 fusion.59
  115.5 1.1 fusion.60
  116.6 0.8 fusion.59
  118.1 1.1 fusion.60
  119.2 0.8 fusion.59
  120.7 1.1 fusion.60
  121.8 0.8 fusion.59
  123.3 1.1 fusion.60
  124.4 0.8 fusion.59
  125.9 1.1 fusion.60
  127.0 0.8 fusion.59
  128.6 1.1 fusion.60
  129.6 0.8 fusion.59
  131.2 1.1 fusion.60
  132.7 2.0 fusion.35
  134.7 88.3 %all-reduce.5.cloned.1.call-done = f32[32,2048]{1,0:T(8,128)} async-done(((f32[32,2048]{1,0:T(8,128)}), f32[32,2048]{1,0:T(8,128)}) %all-reduce.5.cloned.1.call-update) | async-done | bytes 262160
  223.0 1.0 multiply_reduce_fusion
  224.0 0.9 fusion.37
  224.9 21.2 %all-gather.2 = bf16[16,2,2048]{2,1,0:T(2,128)(2,1)S(1)} all-gather(bf16[1,2,2048]{2,1,0:T(2,128)(2,1)S(1)} %fusion.37), channel_id=1, replica_groups=mesh['groups'=2,'seq'=16] {'seq'}, dimensions={0}, use_global_device_ids=true | all-gather | bytes 139264 | tf_op jit(solution)/shard_map/all_gather | solution.py:103
  246.2 3.3 fusion.27
  249.5 0.3 fusion.5
  249.9 1.0 copy.46
  250.9 84.8 %all-reduce.7.cloned.1.call-done = f32[32,2048]{1,0:T(8,128)} async-done(((f32[32,2048]{1,0:T(8,128)}), f32[32,2048]{1,0:T(8,128)}) %all-reduce.7.cloned.1.call-update) | async-done | bytes 262160
  335.6 1.5 fusion.34
  (90 shorter events, 12.3 us)
Async XLA Ops:
  7.2 239.0 %copy-start = (bf16[512,2048]{1,0:T(8,128)(2,1)S(1)}, bf16[512,2048]{1,0:T(8,128)(2,1)}, u32[]{:S(2)}) copy-start(bf16[512,2048]{1,0:T(8,128)(2,1)} %param.15) | copy-start | bytes 6291460
  7.2 2.5 copy-start.6
  7.2 84.8 %all-gather.5.cloned.1.call-start = ((), (), s32[]{:S(2)}) async-start(), calls=%async_computation | async-start | bytes 4456448 | tf_op jit(solution)/shard_map/all_gather | solution.py:16
  42.1 180.9 %all-reduce.5.cloned.1.call-start = ((), (), s32[]{:S(2)}) async-start(), calls=%async_computation.1 | async-start | bytes 524288
  65.4 0.7 copy-start.3
  91.0 0.8 copy-start.1
  132.2 90.7 %copy-start.5 = (bf16[2,2048]{1,0:T(2,128)(2,1)S(1)}, bf16[2,2048]{1,0:T(2,128)(2,1)}, u32[]{:S(2)}) copy-start(bf16[2,2048]{1,0:T(2,128)(2,1)} %param.9) | copy-start | bytes 24580
  132.3 91.7 %copy-start.7 = (f32[2048]{0:T(1024)S(1)}, f32[2048]{0:T(1024)}, u32[]{:S(2)}) copy-start(f32[2048]{0:T(1024)} %param.13) | copy-start | bytes 24580
  134.6 201.0 %all-reduce.7.cloned.1.call-start = ((), (), s32[]{:S(2)}) async-start(), calls=%async_computation.2 | async-start | bytes 524288
  246.2 3.3 copy-start.2
  246.2 3.3 copy-start.4
Sparse Core Ops, SparseCore 0:
  42.2 49.7 all-gather.4
  134.8 88.1 all-reduce.4
  249.6 85.9 all-reduce.6
where the time goes:
time: 347 us; the launch traced here: 344 us
  waiting for transfers between devices  173 us (50%)
  blocking collectives  86.5 us (25%)
  other arithmetic  31.2 us (9%)
  local copies, waits for them, and re-layouts  29.8 us (9%)
  between operations  14.6 us (4%)
  matrix products  7.7 us (2%)
    unnamed x5, waiting for transfers between devices  173 us
    all_gather x2, blocking collectives, joined_2(): gathered = jax.tree.map(lambda a: lax.all_gather(a, axis), part)  40.7 us
    all_gather x1, blocking collectives, local(): gathered = lax.all_gather(audio_qkv, 'seq', axis=1, tiled=True)  24.6 us
    all_gather x1, blocking collectives, local(): lax.all_gather(normed, 'seq', axis=0, tiled=True)  21.2 us
    add x15, other arithmetic, combine(): joined = (left_sum + right_sum).reshape(earlier[2].shape)  15.9 us
    add x15, other arithmetic, combine(): return (highest, earlier[1] * left_scale + later[1] * right_scale, joined)  11.4 us
  transfers between devices with their start and end apart: 3, of which 3 were waited for; matrix products, arithmetic and copies ran while one was open for 2% of the time, Pallas kernels for 0%

commit v1 on v0

v1 whole, which is shorter than its diff:
```python
import functools
import math

import jax
import jax.numpy as jnp
from jax import lax
from jax.experimental import pallas as pl
from jax.experimental.pallas import tpu as pltpu
from jax.sharding import PartitionSpec as P

HEADS = 32
HD = 64
LANES = 128
STATS = 16
EPSILON = 1e-06
SCALE = 1.0 / math.sqrt(HD)
F32 = jnp.float32
BF16 = jnp.bfloat16


def mm(a, b, ca, cb):
    return lax.dot_general(a, b, (((ca,), (cb,)), ((), ())), preferred_element_type=F32)


def lane_of(shape):
    return lax.broadcasted_iota(jnp.int32, shape, len(shape) - 1)


def kernel(
    n, stream, aqkv, vqkv, wo, gain, w1, w2,
    vmix_out, result,
    vq, vk, vv, vt, wo_v, w1_v, w2_v, vmix,
    relay, relay_own, qmat, kmat, vmat,
    g_q, g_kv, p_send, p_recv, a_send, a_recv, g_n, o_send, o_recv,
    load_sem, out_sem, send_sem, recv_sem,
):
    me = lax.axis_index("seq")
    tokens, width = stream.shape
    chunks = width // LANES
    block = tokens * chunks
    audio = n * tokens
    group = LANES // audio
    window = max(group * HD, LANES)
    windows = width // window
    subs = window // (group * HD)
    slab = wo.shape[0]
    receivers = n // (windows * subs)
    rows = HD // receivers

    def peer_of(i):
        return lax.rem(me + 1 + lax.rem(i + n // 2 - 1, n - 1), n)

    def remote(src, dst, phase, peer):
        return pltpu.make_async_remote_copy(
            src_ref=src,
            dst_ref=dst,
            send_sem=send_sem.at[phase],
            recv_sem=recv_sem.at[phase],
            device_id={"seq": peer},
            device_id_type=pl.DeviceIdType.MESH,
        )

    def each_peer(act):
        def body(i, carry):
            act(peer_of(i))
            return carry

        lax.fori_loop(0, n - 1, body, 0)

    def all_of(ref, phase):
        part = ref.at[pl.ds(0, n - 1)]
        return remote(part, part, phase, lax.rem(me + 1, n))

    barrier = pltpu.get_barrier_semaphore()
    each_peer(
        lambda peer: pl.semaphore_signal(
            barrier, inc=1, device_id={"seq": peer}, device_id_type=pl.DeviceIdType.MESH
        )
    )

    sources = (vqkv.at[1], vqkv.at[2], vqkv.at[0], wo, w1, w2)
    places = (vk, vv, vq, wo_v, w1_v, w2_v)
    loads = [
        pltpu.make_async_copy(src, dst, load_sem.at[i])
        for i, (src, dst) in enumerate(zip(sources, places))
    ]
    for load in loads:
        load.start()

    def own_blocks(value):
        for c in range(chunks):
            relay_own[pl.ds(c, tokens, stride=chunks), :] = value[:, c * LANES : (c + 1) * LANES]
        return relay_own[...]

    g_q[me] = (own_blocks(aqkv[0].astype(F32)) * SCALE).astype(BF16)
    g_kv[me, 0:block] = (own_blocks(aqkv[1].astype(F32)) * SCALE).astype(BF16)
    g_kv[me, block : 2 * block] = own_blocks(aqkv[2].astype(F32)).astype(BF16)

    pl.semaphore_wait(barrier, n - 1)
    each_peer(lambda peer: remote(g_q.at[me], g_q.at[me], 0, peer).start())
    each_peer(lambda peer: remote(g_kv.at[me], g_kv.at[me], 1, peer).start())

    def rows_of(blocks):
        relay[...] = blocks.astype(F32).reshape(audio * chunks, LANES)
        return jnp.concatenate(
            [relay[pl.ds(c, audio, stride=chunks), :].astype(BF16) for c in range(chunks)], axis=1
        )

    def blocks_of(value):
        for c in range(chunks):
            relay[pl.ds(c, audio, stride=chunks), :] = value[:, c * LANES : (c + 1) * LANES]
        return relay[...].astype(BF16).reshape(n, block, LANES)

    def diagonal(part, sub):
        head = lane_of(part.shape) // HD
        return jnp.concatenate(
            [jnp.where(head == sub * group + h, part, jnp.zeros_like(part)) for h in range(group)],
            axis=0,
        )

    loads[0].wait()
    loads[1].wait()
    for w in range(windows):
        cols = slice(w * window, (w + 1) * window)
        vt[cols, :] = vv[:, cols].T

    all_of(g_q, 0).wait_recv()
    qmat[...] = rows_of(g_q[...])

    for w in range(windows):
        cols = slice(w * window, (w + 1) * window)
        for sub in range(subs):
            scores = mm(vk[:, cols], diagonal(qmat[:, cols], sub), 1, 1)
            peak = jnp.max(scores, axis=0, keepdims=True).astype(BF16).astype(F32)
            weights = jnp.exp(scores - peak)
            total = jnp.sum(weights, axis=0, keepdims=True)
            product = mm(vt[cols, :], weights.astype(BF16), 1, 0)
            lane = lane_of((HD, LANES)) // audio
            chosen = jnp.zeros((HD, LANES), F32)
            for h in range(group):
                at = (sub * group + h) * HD
                chosen = jnp.where(lane == h, product[at : at + HD], chosen)
            high = total.astype(BF16).astype(F32)
            row = lax.broadcasted_iota(jnp.int32, (STATS, LANES), 0)
            stats = jnp.where(
                row == 0, peak, jnp.where(row == 1, high, jnp.where(row == 2, total - high, 0.0))
            )
            for j in range(receivers):
                if slab < HD:
                    numerator, mine = chosen[j * rows : (j + 1) * rows], stats
                else:
                    span = slab // HD * audio
                    numerator, mine = jnp.zeros((rows, LANES), F32), jnp.zeros((STATS, LANES), F32)
                    for i in range(LANES // span):
                        shift = (i - j) * span % LANES
                        part, part_stats = chosen[i * rows : (i + 1) * rows], stats
                        if shift:
                            part = pltpu.roll(part, shift, 1)
                            part_stats = pltpu.roll(part_stats, shift, 1)
                        numerator = jnp.where(
                            lane_of((rows, LANES)) // span == i, part, numerator
                        )
                        mine = jnp.where(lane_of((STATS, LANES)) // span == i, part_stats, mine)
                target = (w * subs + sub) * receivers + j
                p_send[target, 0:rows] = numerator.astype(BF16)
                p_send[target, rows : rows + STATS] = mine.astype(BF16)

                @pl.when(me != target)
                def _():
                    remote(p_send.at[target], p_recv.at[me], 2, target).start()

    p_recv[me] = p_send[me]

    all_of(g_kv, 1).wait_recv()
    loads[2].wait()
    kmat[...] = rows_of(g_kv[:, 0:block])
    vmat[...] = rows_of(g_kv[:, block : 2 * block])
    store = pltpu.make_async_copy(vmix, vmix_out, out_sem)

    def video(first, last):
        for w in range(first, last):
            cols = slice(w * window, (w + 1) * window)
            mixed = None
            for sub in range(subs):
                scores = mm(diagonal(kmat[:, cols], sub), vq[:, cols], 1, 1)
                scores = scores.reshape(group, audio, scores.shape[1])
                weights = jnp.exp(scores - jnp.max(scores, axis=1, keepdims=True))
                weights = weights / jnp.sum(weights, axis=1, keepdims=True)
                weights = weights.reshape(group * audio, scores.shape[2])
                term = mm(weights.T.astype(BF16), diagonal(vmat[:, cols], sub), 1, 0)
                mixed = term if mixed is None else mixed + term
            vmix[:, cols] = mixed.astype(BF16)

    video(0, windows)
    store.start()

    all_of(p_recv, 2).wait_recv()
    loads[3].wait()
    parts = p_recv[...].astype(F32)
    peaks = parts[:, rows : rows + 1]
    scales = jnp.exp(peaks - jnp.max(peaks, axis=0, keepdims=True))
    totals = (parts[:, rows + 1 : rows + 2] + parts[:, rows + 2 : rows + 3]) * scales
    attended = jnp.sum(parts[:, 0:rows] * scales, axis=0) / jnp.sum(totals, axis=0)
    turned = attended.T.astype(BF16)
    if slab < HD:
        columns = turned
    else:
        heads = slab // HD
        folds = HD // rows
        columns = jnp.concatenate(
            [
                turned[(f * heads + h) * audio : (f * heads + h + 1) * audio]
                for h in range(heads)
                for f in range(folds)
            ],
            axis=1,
        )

    def scatter(value, send, recv, phase):
        send[...] = blocks_of(value)
        each_peer(lambda peer: remote(send.at[peer], recv.at[me], phase, peer).start())
        recv[me] = send[me]

    scatter(mm(columns, wo_v[...], 1, 0), a_send, a_recv, 3)
    own = own_blocks(stream[...].astype(F32))
    all_of(a_recv, 3).wait_recv()
    mixed_audio = own + jnp.sum(a_recv[...].astype(F32), axis=0)

    by_token = mixed_audio.reshape(tokens, chunks, LANES)
    square = jnp.sum(jnp.sum(by_token * by_token, axis=1, keepdims=True), axis=2, keepdims=True)
    normed = by_token * lax.rsqrt(square / width + EPSILON) * gain[...][None]
    g_n[me] = normed.reshape(block, LANES).astype(BF16)
    each_peer(lambda peer: remote(g_n.at[me], g_n.at[me], 4, peer).start())
    loads[4].wait()
    loads[5].wait()
    all_of(g_n, 4).wait_recv()

    hidden = jax.nn.gelu(mm(rows_of(g_n[...]), w1_v[...], 1, 0), approximate=True)
    scatter(mm(hidden.astype(BF16), w2_v[...], 1, 0), o_send, o_recv, 5)
    all_of(o_recv, 5).wait_recv()
    relay_own[...] = mixed_audio + jnp.sum(o_recv[...].astype(F32), axis=0)
    for c in range(chunks):
        result[:, c * LANES : (c + 1) * LANES] = relay_own[
            pl.ds(c, tokens, stride=chunks), :
        ].astype(BF16)

    for phase, ref in enumerate((g_q, g_kv, p_send, a_send, g_n, o_send)):
        all_of(ref, phase).wait_send()
    store.wait()


def local(n, audio_stream, audio_qkv, video_qkv, attention_out, norm_gain, weight_in, weight_out):
    tokens, width = audio_stream.shape
    chunks = width // LANES
    block = tokens * chunks
    audio = n * tokens
    video = video_qkv.shape[1]
    receivers = n * LANES // (audio * HEADS)
    part = HD // receivers + STATS
    vmem = pl.BlockSpec(memory_space=pltpu.VMEM)
    anywhere = pl.BlockSpec(memory_space=pl.ANY)
    gathered = pltpu.VMEM((n, block, LANES), BF16)
    parts = pltpu.VMEM((n, part, LANES), BF16)
    return pl.pallas_call(
        functools.partial(kernel, n),
        out_shape=(
            jax.ShapeDtypeStruct((video, width), BF16),
            jax.ShapeDtypeStruct((tokens, width), BF16),
        ),
        in_specs=[vmem, vmem, anywhere, anywhere, vmem, anywhere, anywhere],
        out_specs=(anywhere, vmem),
        scratch_shapes=[
            pltpu.VMEM((video, width), BF16),
            pltpu.VMEM((video, width), BF16),
            pltpu.VMEM((video, width), BF16),
            pltpu.VMEM((width, video), BF16),
            pltpu.VMEM(attention_out.shape, BF16),
            pltpu.VMEM(weight_in.shape, BF16),
            pltpu.VMEM(weight_out.shape, BF16),
            pltpu.VMEM((video, width), BF16),
            pltpu.VMEM((audio * chunks, LANES), F32),
            pltpu.VMEM((block, LANES), F32),
            pltpu.VMEM((audio, width), BF16),
            pltpu.VMEM((audio, width), BF16),
            pltpu.VMEM((audio, width), BF16),
            gathered,
            pltpu.VMEM((n, 2 * block, LANES), BF16),
            parts,
            parts,
            gathered,
            gathered,
            gathered,
            gathered,
            gathered,
            pltpu.SemaphoreType.DMA((6,)),
            pltpu.SemaphoreType.DMA,
            pltpu.SemaphoreType.DMA((6,)),
            pltpu.SemaphoreType.DMA((6,)),
        ],
        compiler_params=pltpu.CompilerParams(
            collective_id=0, has_side_effects=True, vmem_limit_bytes=48 * 1024 * 1024
        ),
        name="cross_modal_layer",
    )(
        audio_stream,
        audio_qkv,
        video_qkv,
        attention_out,
        norm_gain.reshape(chunks, LANES),
        weight_in,
        weight_out,
    )


def solution(mesh):
    placed = (
        P(("groups", "seq"), None),
        P(None, ("groups", "seq"), None),
        P(None, ("groups", "seq"), None),
        P("seq", None),
        P(),
        P(None, "seq"),
        P("seq", None),
    )
    return jax.shard_map(
        functools.partial(local, mesh.shape["seq"]),
        mesh=mesh,
        in_specs=placed,
        out_specs=(P(("groups", "seq"), None), P(("groups", "seq"), None)),
        check_vma=False,
    )
```

time: 347 us -> 46.9 us (0.14)
  waiting for transfers between devices: 173 us -> 0 us
  blocking collectives: 86.5 us -> 0 us
  Pallas kernels: 0 us -> 38.3 us
  other arithmetic: 31.2 us -> 0 us
  local copies, waits for them, and re-layouts: 29.8 us -> 7.56 us
  between operations: 14.6 us -> 0.65 us
  matrix products: 7.7 us -> 0 us
    unnamed x5 -> x0, waiting for transfers between devices: 173 us -> none
    all_gather x4 -> x0, blocking collectives: 86.5 us -> none  [the longest x2 40.7 us: joined_2(): gathered = jax.tree.map(lambda a: lax.all_gather(a, axis), part)]
    pallas_call x0 -> x1, Pallas kernels: none -> 38.3 us  [local(): pl.pallas_call(functools.partial(kernel, n), out_shape=(jax.ShapeDtypeStr...]
    add x30 -> x0, other arithmetic: 27.3 us -> none  [the longest x15 15.9 us: combine(): joined = (left_sum + right_sum).reshape(earlier[2].shape)]
    mul x60 -> x0, local copies, waits for them, and re-layouts: 11.3 us -> none  [the longest x30 5.69 us: combine(): left_sum = head_view(earlier[2]) * left_scale[:, :, None]]
    dot_general x6 -> x0, matrix products: 7.7 us -> none  [the longest x1 3.28 us: local(): jnp.dot(hidden, weight_out, preferred_element_type=jnp.float32)]
    slice x5 -> x0, local copies, waits for them, and re-layouts: 7.3 us -> none  [the longest x2 2.69 us: local(): numerator = weighted(weights, video_qkv[2]).reshape(audio_count, HEADS * HD)]
    another operation x4 -> x0, local copies, waits for them, and re-layouts: 4.19 us -> none  [the longest x3 3.3 us: head_view(): return block.reshape(block.shape[0], HEADS, HD)]
  transfers between devices with their start and end apart: 3 -> 0, of which waited for: 3 -> 0; matrix products, arithmetic and copies ran while one was open for 2% -> 0% of each run, Pallas kernels for 0% -> 0%
where the time goes in v1:
time: 46.9 us; the launch traced here: 46.5 us
  Pallas kernels  38.3 us (82%)
  local copies, waits for them, and re-layouts  7.56 us (16%)
  between operations  0.65 us (1%)
    pallas_call x1, Pallas kernels, local(): pl.pallas_call(functools.partial(kernel, n), out_shape=(jax.ShapeDtypeStr...  38.3 us
    unnamed x14, local copies, waits for them, and re-layouts  7.56 us

profile of v1, /device:TPU:0, one launch (start us, length us, event | category | flops | bytes accessed | tf_op | source)
XLA Modules:
  0.0 46.5 jit_solution(1508634912199509609)
XLA Ops:
  0.6 0.0 copy-start
  0.6 1.6 %copy-done = bf16[2048,512]{1,0:T(8,128)(2,1)S(1)} copy-done((bf16[2048,512]{1,0:T(8,128)(2,1)S(1)}, bf16[2048,512]{1,0:T(8,128)(2,1)}, u32[]{:S(2)}) %copy-start) | copy-done | bytes 2097176
  2.2 0.0 copy-start.1
  2.2 1.4 %copy-done.1 = bf16[3,128,2048]{2,1,0:T(8,128)(2,1)S(1)} copy-done((bf16[3,128,2048]{2,1,0:T(8,128)(2,1)S(1)}, bf16[3,128,2048]{2,1,0:T(8,128)(2,1)}, u32[]{:S(2)}) %copy-start.1) | copy-done | bytes 1572888
  3.6 0.0 copy-start.2
  3.6 1.0 %copy-done.2 = bf16[128,2048]{1,0:T(8,128)(2,1)S(1)} copy-done((bf16[128,2048]{1,0:T(8,128)(2,1)S(1)}, bf16[128,2048]{1,0:T(8,128)(2,1)}, u32[]{:S(2)}) %copy-start.2) | copy-done | bytes 524312
  4.7 0.0 copy-start.3
  4.7 0.7 %copy-done.3 = bf16[3,2,2048]{2,1,0:T(2,128)(2,1)S(1)} copy-done((bf16[3,2,2048]{2,1,0:T(2,128)(2,1)S(1)}, bf16[3,2,2048]{2,1,0:T(2,128)(2,1)}, u32[]{:S(2)}) %copy-start.3) | copy-done | bytes 24600
  5.4 0.0 copy-start.4
  5.4 0.7 %copy-done.4 = bf16[2,2048]{1,0:T(2,128)(2,1)S(1)} copy-done((bf16[2,2048]{1,0:T(2,128)(2,1)S(1)}, bf16[2,2048]{1,0:T(2,128)(2,1)}, u32[]{:S(2)}) %copy-start.4) | copy-done | bytes 8216
  6.1 0.0 copy-start.5
  6.1 0.7 %copy-done.5 = f32[2048]{0:T(1024)S(1)} copy-done((f32[2048]{0:T(1024)S(1)}, f32[2048]{0:T(1024)}, u32[]{:S(2)}) %copy-start.5) | copy-done | bytes 8216
  6.8 38.3 %cross_modal_layer.1 = (bf16[128,2048]{1,0:T(8,128)(2,1)S(1)}, bf16[2,2048]{1,0:T(2,128)(2,1)S(1)}) custom-call(bf16[2,2048]{1,0:T(2,128)(2,1)S(1)} %copy-done.4, bf16[3,2,2048]{2,1,0:T(2,128)(2,1)S(1)} %copy-done.3, bf16[3,128,2048]{2,1,0:T(8,128)(2,1)S(1)} %copy-done.1, bf16[128,2048]{1,0:T(8,128)(2,1)S(1)} %copy-done.2, f32[16,128]{1,0:T(8,128)S(1)} %bitcast.1, ...), custom_call_target="tpu_custom_call" | custom-call | tf_op jit(solution)/shard_map/cross_modal_layer/pallas_call | solution.py:264
  45.1 0.8 %copy.11 = bf16[128,2048]{1,0:T(8,128)(2,1)} copy(bf16[128,2048]{1,0:T(8,128)(2,1)S(1)} %get-tuple-element.4) | data formatting | bytes 1048576
  45.9 0.6 %copy.12 = bf16[2,2048]{1,0:T(2,128)(2,1)} copy(bf16[2,2048]{1,0:T(2,128)(2,1)S(1)} %get-tuple-element.5) | data formatting | bytes 16384
Async XLA Ops:
  0.6 1.6 %copy-start = (bf16[2048,512]{1,0:T(8,128)(2,1)S(1)}, bf16[2048,512]{1,0:T(8,128)(2,1)}, u32[]{:S(2)}) copy-start(bf16[2048,512]{1,0:T(8,128)(2,1)} %w1.1) | copy-start | bytes 6291460
  2.2 1.4 %copy-start.1 = (bf16[3,128,2048]{2,1,0:T(8,128)(2,1)S(1)}, bf16[3,128,2048]{2,1,0:T(8,128)(2,1)}, u32[]{:S(2)}) copy-start(bf16[3,128,2048]{2,1,0:T(8,128)(2,1)} %vqkv.1) | copy-start | bytes 4718596
  3.6 1.0 %copy-start.2 = (bf16[128,2048]{1,0:T(8,128)(2,1)S(1)}, bf16[128,2048]{1,0:T(8,128)(2,1)}, u32[]{:S(2)}) copy-start(bf16[128,2048]{1,0:T(8,128)(2,1)} %wo.1) | copy-start | bytes 1572868
  4.7 0.7 %copy-start.3 = (bf16[3,2,2048]{2,1,0:T(2,128)(2,1)S(1)}, bf16[3,2,2048]{2,1,0:T(2,128)(2,1)}, u32[]{:S(2)}) copy-start(bf16[3,2,2048]{2,1,0:T(2,128)(2,1)} %aqkv.1) | copy-start | bytes 73732
  5.4 0.7 %copy-start.4 = (bf16[2,2048]{1,0:T(2,128)(2,1)S(1)}, bf16[2,2048]{1,0:T(2,128)(2,1)}, u32[]{:S(2)}) copy-start(bf16[2,2048]{1,0:T(2,128)(2,1)} %stream.1) | copy-start | bytes 24580
  6.1 0.7 %copy-start.5 = (f32[2048]{0:T(1024)S(1)}, f32[2048]{0:T(1024)}, u32[]{:S(2)}) copy-start(f32[2048]{0:T(1024)} %param.11) | copy-start | bytes 24580

commit v2 on v1

--- a/solution.py
+++ b/solution.py
@@ -12,6 +12,7 @@
 HD = 64
 LANES = 128
 STATS = 16
+NEAR = 4
 EPSILON = 1e-06
 SCALE = 1.0 / math.sqrt(HD)
 F32 = jnp.float32
@@ -27,9 +28,9 @@
 
 
 def kernel(
-    n, stream, aqkv, vqkv, wo, gain, w1, w2,
+    n, near, stream_in, aqkv_in, vqkv, wo, gain_in, w1, w2,
     vmix_out, result,
-    vq, vk, vv, vt, wo_v, w1_v, w2_v, vmix,
+    stream, aqkv, gain, vq, vk, vv, vt, wo_v, w1_v, w2_v, vmix,
     relay, relay_own, qmat, kmat, vmat,
     g_q, g_kv, p_send, p_recv, a_send, a_recv, g_n, o_send, o_recv,
     load_sem, out_sem, send_sem, recv_sem,
@@ -47,9 +48,6 @@
     receivers = n // (windows * subs)
     rows = HD // receivers
 
-    def peer_of(i):
-        return lax.rem(me + 1 + lax.rem(i + n // 2 - 1, n - 1), n)
-
     def remote(src, dst, phase, peer):
         return pltpu.make_async_remote_copy(
             src_ref=src,
@@ -61,14 +59,11 @@
         )
 
     def each_peer(act):
-        def body(i, carry):
-            act(peer_of(i))
-            return carry
-
-        lax.fori_loop(0, n - 1, body, 0)
-
-    def all_of(ref, phase):
-        part = ref.at[pl.ds(0, n - 1)]
+        for i in range(n - 1):
+            act(lax.rem(me + 1 + (i + n // 2 - 1) % (n - 1), n))
+
+    def all_of(ref, phase, count=n - 1):
+        part = ref.at[pl.ds(0, count)]
         return remote(part, part, phase, lax.rem(me + 1, n))
 
     barrier = pltpu.get_barrier_semaphore()
@@ -78,8 +73,8 @@
         )
     )
 
-    sources = (vqkv.at[1], vqkv.at[2], vqkv.at[0], wo, w1, w2)
-    places = (vk, vv, vq, wo_v, w1_v, w2_v)
+    sources = (aqkv_in, vqkv.at[1], vqkv.at[2], vqkv.at[0], wo, stream_in, gain_in, w1, w2)
+    places = (aqkv, vk, vv, vq, wo_v, stream, gain, w1_v, w2_v)
     loads = [
         pltpu.make_async_copy(src, dst, load_sem.at[i])
         for i, (src, dst) in enumerate(zip(sources, places))
@@ -92,13 +87,30 @@
             relay_own[pl.ds(c, tokens, stride=chunks), :] = value[:, c * LANES : (c + 1) * LANES]
         return relay_own[...]
 
+    far = n // near
+    my_far, my_near = lax.div(me, near), lax.rem(me, near)
+    kv_slot = my_near * far + my_far
+    kv_row = pl.ds(my_near * far, far)
+
+    def kv_across():
+        for i in range(1, far):
+            peer = lax.rem(my_far + i, far) * near + my_near
+            remote(g_kv.at[kv_slot], g_kv.at[kv_slot], 1, peer).start()
+
+    def kv_within():
+        all_of(g_kv, 1, far - 1).wait_recv()
+        for i in range(1, near):
+            peer = my_far * near + lax.rem(my_near + i, near)
+            remote(g_kv.at[kv_row], g_kv.at[kv_row], 6, peer).start()
+
+    loads[0].wait()
     g_q[me] = (own_blocks(aqkv[0].astype(F32)) * SCALE).astype(BF16)
-    g_kv[me, 0:block] = (own_blocks(aqkv[1].astype(F32)) * SCALE).astype(BF16)
-    g_kv[me, block : 2 * block] = own_blocks(aqkv[2].astype(F32)).astype(BF16)
+    g_kv[kv_slot, 0:block] = (own_blocks(aqkv[1].astype(F32)) * SCALE).astype(BF16)
+    g_kv[kv_slot, block : 2 * block] = own_blocks(aqkv[2].astype(F32)).astype(BF16)
 
     pl.semaphore_wait(barrier, n - 1)
     each_peer(lambda peer: remote(g_q.at[me], g_q.at[me], 0, peer).start())
-    each_peer(lambda peer: remote(g_kv.at[me], g_kv.at[me], 1, peer).start())
+    kv_across()
 
     def rows_of(blocks):
         relay[...] = blocks.astype(F32).reshape(audio * chunks, LANES)
@@ -118,8 +130,8 @@
             axis=0,
         )
 
-    loads[0].wait()
     loads[1].wait()
+    loads[2].wait()
     for w in range(windows):
         cols = slice(w * window, (w + 1) * window)
         vt[cols, :] = vv[:, cols].T
@@ -165,16 +177,10 @@
                 p_send[target, 0:rows] = numerator.astype(BF16)
                 p_send[target, rows : rows + STATS] = mine.astype(BF16)
 
-                @pl.when(me != target)
-                def _():
-                    remote(p_send.at[target], p_recv.at[me], 2, target).start()
-
+    each_peer(lambda peer: remote(p_send.at[peer], p_recv.at[me], 2, peer).start())
+    kv_within()
     p_recv[me] = p_send[me]
 
-    all_of(g_kv, 1).wait_recv()
-    loads[2].wait()
-    kmat[...] = rows_of(g_kv[:, 0:block])
-    vmat[...] = rows_of(g_kv[:, block : 2 * block])
     store = pltpu.make_async_copy(vmix, vmix_out, out_sem)
 
     def video(first, last):
@@ -191,11 +197,8 @@
                 mixed = term if mixed is None else mixed + term
             vmix[:, cols] = mixed.astype(BF16)
 
-    video(0, windows)
-    store.start()
-
     all_of(p_recv, 2).wait_recv()
-    loads[3].wait()
+    loads[4].wait()
     parts = p_recv[...].astype(F32)
     peaks = parts[:, rows : rows + 1]
     scales = jnp.exp(peaks - jnp.max(peaks, axis=0, keepdims=True))
@@ -222,7 +225,14 @@
         recv[me] = send[me]
 
     scatter(mm(columns, wo_v[...], 1, 0), a_send, a_recv, 3)
+    loads[5].wait()
+    loads[6].wait()
     own = own_blocks(stream[...].astype(F32))
+    all_of(g_kv, 6, far * (near - 1)).wait_recv()
+    loads[3].wait()
+    kmat[...] = rows_of(g_kv[:, 0:block])
+    vmat[...] = rows_of(g_kv[:, block : 2 * block])
+    video(0, windows // 2)
     all_of(a_recv, 3).wait_recv()
     mixed_audio = own + jnp.sum(a_recv[...].astype(F32), axis=0)
 
@@ -231,8 +241,10 @@
     normed = by_token * lax.rsqrt(square / width + EPSILON) * gain[...][None]
     g_n[me] = normed.reshape(block, LANES).astype(BF16)
     each_peer(lambda peer: remote(g_n.at[me], g_n.at[me], 4, peer).start())
-    loads[4].wait()
-    loads[5].wait()
+    video(windows // 2, windows)
+    store.start()
+    loads[7].wait()
+    loads[8].wait()
     all_of(g_n, 4).wait_recv()
 
     hidden = jax.nn.gelu(mm(rows_of(g_n[...]), w1_v[...], 1, 0), approximate=True)
@@ -244,7 +256,9 @@
             pl.ds(c, tokens, stride=chunks), :
         ].astype(BF16)
 
-    for phase, ref in enumerate((g_q, g_kv, p_send, a_send, g_n, o_send)):
+    all_of(g_kv, 1, far - 1).wait_send()
+    all_of(g_kv, 6, far * (near - 1)).wait_send()
+    for phase, ref in ((0, g_q), (2, p_send), (3, a_send), (4, g_n), (5, o_send)):
         all_of(ref, phase).wait_send()
     store.wait()
 
@@ -258,18 +272,21 @@
     receivers = n * LANES // (audio * HEADS)
     part = HD // receivers + STATS
     vmem = pl.BlockSpec(memory_space=pltpu.VMEM)
-    anywhere = pl.BlockSpec(memory_space=pl.ANY)
+    anywhere = pl.BlockSpec(memory_space=pltpu.HBM)
     gathered = pltpu.VMEM((n, block, LANES), BF16)
     parts = pltpu.VMEM((n, part, LANES), BF16)
     return pl.pallas_call(
-        functools.partial(kernel, n),
+        functools.partial(kernel, n, math.gcd(n, NEAR)),
         out_shape=(
             jax.ShapeDtypeStruct((video, width), BF16),
             jax.ShapeDtypeStruct((tokens, width), BF16),
         ),
-        in_specs=[vmem, vmem, anywhere, anywhere, vmem, anywhere, anywhere],
+        in_specs=[anywhere] * 7,
         out_specs=(anywhere, vmem),
         scratch_shapes=[
+            pltpu.VMEM(audio_stream.shape, BF16),
+            pltpu.VMEM(audio_qkv.shape, BF16),
+            pltpu.VMEM((chunks, LANES), F32),
             pltpu.VMEM((video, width), BF16),
             pltpu.VMEM((video, width), BF16),
             pltpu.VMEM((video, width), BF16),
@@ -292,13 +309,13 @@
             gathered,
             gathered,
             gathered,
-            pltpu.SemaphoreType.DMA((6,)),
+            pltpu.SemaphoreType.DMA((9,)),
             pltpu.SemaphoreType.DMA,
-            pltpu.SemaphoreType.DMA((6,)),
-            pltpu.SemaphoreType.DMA((6,)),
+            pltpu.SemaphoreType.DMA((7,)),
+            pltpu.SemaphoreType.DMA((7,)),
         ],
         compiler_params=pltpu.CompilerParams(
-            collective_id=0, has_side_effects=True, vmem_limit_bytes=48 * 1024 * 1024
+            collective_id=0, has_side_effects=True, vmem_limit_bytes=60 * 1024 * 1024
         ),
         name="cross_modal_layer",
     )(

time: 46.9 us -> 40.5 us (0.86)
  local copies, waits for them, and re-layouts: 7.56 us -> 3.18 us
  Pallas kernels: 38.3 us -> 36.5 us
    unnamed x14 -> x2, local copies, waits for them, and re-layouts: 7.56 us -> 3.18 us
    pallas_call x1, Pallas kernels: 38.3 us -> 36.5 us  [local(): pl.pallas_call(functools.partial(kernel, n, math.gcd(n, NEAR)), out_shape...]
where the time goes in v2:
time: 40.5 us; the launch traced here: 40.3 us
  Pallas kernels  36.5 us (90%)
  local copies, waits for them, and re-layouts  3.18 us (8%)
  between operations  0.64 us (2%)
    pallas_call x1, Pallas kernels, local(): pl.pallas_call(functools.partial(kernel, n, math.gcd(n, NEAR)), out_shape...  36.5 us
    unnamed x2, local copies, waits for them, and re-layouts  3.18 us

profile of v2, /device:TPU:0, one launch (start us, length us, event | category | flops | bytes accessed | tf_op | source)
XLA Modules:
  0.0 40.3 jit_solution(14660930301038863539)
XLA Ops:
  0.6 36.5 %cross_modal_layer.1 = (bf16[128,2048]{1,0:T(8,128)(2,1)}, bf16[2,2048]{1,0:T(2,128)(2,1)}) custom-call(bf16[2,2048]{1,0:T(2,128)(2,1)} %stream_in.1, bf16[3,2,2048]{2,1,0:T(2,128)(2,1)} %aqkv_in.1, bf16[3,128,2048]{2,1,0:T(8,128)(2,1)} %vqkv.1, bf16[128,2048]{1,0:T(8,128)(2,1)} %wo.1, f32[16,128]{1,0:T(8,128)} %bitcast.1, bf16[2048,512]{1,0:T(8,128)(2,1)} %w1.1, ...), custom_call_target="tpu_custom_call" | custom-call | tf_op jit(solution)/shard_map/cross_modal_layer/pallas_call | solution.py:278
  37.1 1.9 %copy.11 = bf16[128,2048]{1,0:T(8,128)(2,1)} copy(bf16[128,2048]{1,0:T(8,128)(2,1)} %get-tuple-element.4) | data formatting | bytes 1048576
  39.0 1.3 %copy.12 = bf16[2,2048]{1,0:T(2,128)(2,1)} copy(bf16[2,2048]{1,0:T(2,128)(2,1)} %get-tuple-element.5) | data formatting | bytes 16384

commit v3 on v2

--- a/solution.py
+++ b/solution.py
@@ -13,6 +13,7 @@
 LANES = 128
 STATS = 16
 NEAR = 4
+PIECES = 4
 EPSILON = 1e-06
 SCALE = 1.0 / math.sqrt(HD)
 F32 = jnp.float32
@@ -32,7 +33,7 @@
     vmix_out, result,
     stream, aqkv, gain, vq, vk, vv, vt, wo_v, w1_v, w2_v, vmix,
     relay, relay_own, qmat, kmat, vmat,
-    g_q, g_kv, p_send, p_recv, a_send, a_recv, g_n, o_send, o_recv,
+    q_send, g_q, g_kv, p_send, p_recv, a_send, a_recv, g_n, o_send, o_recv,
     load_sem, out_sem, send_sem, recv_sem,
 ):
     me = lax.axis_index("seq")
@@ -73,8 +74,18 @@
         )
     )
 
-    sources = (aqkv_in, vqkv.at[1], vqkv.at[2], vqkv.at[0], wo, stream_in, gain_in, w1, w2)
-    places = (aqkv, vk, vv, vq, wo_v, stream, gain, w1_v, w2_v)
+    core = lax.rem(me, 2)
+    chip = lax.div(me, 2)
+    partner = me + 1 - 2 * core
+    half = n // 2
+    wide = width // 2
+    mine = pl.ds(pl.multiple_of(core * wide, LANES), wide)
+    theirs = pl.ds(pl.multiple_of((1 - core) * wide, LANES), wide)
+    keys = vqkv.shape[1]
+    first, second = pl.ds(0, keys), pl.ds(keys, keys)
+
+    sources = (aqkv_in, vqkv.at[1, :, mine], vqkv.at[2, :, mine], vqkv.at[0], wo, stream_in, gain_in, w1, w2)
+    places = (aqkv, vk.at[first], vv.at[first], vq, wo_v, stream, gain, w1_v, w2_v)
     loads = [
         pltpu.make_async_copy(src, dst, load_sem.at[i])
         for i, (src, dst) in enumerate(zip(sources, places))
@@ -104,18 +115,29 @@
             remote(g_kv.at[kv_row], g_kv.at[kv_row], 6, peer).start()
 
     loads[0].wait()
-    g_q[me] = (own_blocks(aqkv[0].astype(F32)) * SCALE).astype(BF16)
+    queries = (own_blocks(aqkv[0].astype(F32)) * SCALE).reshape(tokens, 2, chunks // 2, LANES)
+    for h in range(2):
+        q_send[h] = queries[:, h].reshape(block // 2, LANES).astype(BF16)
+    g_q[me] = q_send[core]
     g_kv[kv_slot, 0:block] = (own_blocks(aqkv[1].astype(F32)) * SCALE).astype(BF16)
     g_kv[kv_slot, block : 2 * block] = own_blocks(aqkv[2].astype(F32)).astype(BF16)
 
     pl.semaphore_wait(barrier, n - 1)
-    each_peer(lambda peer: remote(g_q.at[me], g_q.at[me], 0, peer).start())
+    shared = [
+        remote(vqkv.at[1 + i, :, theirs], ref.at[second], 7 + i, partner)
+        for i, ref in enumerate((vk, vv))
+    ]
+    for copy in shared:
+        copy.start()
+    each_peer(lambda peer: remote(q_send.at[lax.rem(peer, 2)], g_q.at[me], 0, peer).start())
     kv_across()
 
     def rows_of(blocks):
-        relay[...] = blocks.astype(F32).reshape(audio * chunks, LANES)
+        count = blocks.shape[0] * blocks.shape[1]
+        step = count // audio
+        relay[0:count] = blocks.astype(F32).reshape(count, LANES)
         return jnp.concatenate(
-            [relay[pl.ds(c, audio, stride=chunks), :].astype(BF16) for c in range(chunks)], axis=1
+            [relay[pl.ds(c, audio, stride=step), :].astype(BF16) for c in range(step)], axis=1
         )
 
     def blocks_of(value):
@@ -132,14 +154,16 @@
 
     loads[1].wait()
     loads[2].wait()
-    for w in range(windows):
+    for copy in shared:
+        copy.wait_recv()
+    for w in range(windows // 2):
         cols = slice(w * window, (w + 1) * window)
         vt[cols, :] = vv[:, cols].T
 
     all_of(g_q, 0).wait_recv()
     qmat[...] = rows_of(g_q[...])
 
-    for w in range(windows):
+    for w in range(windows // 2):
         cols = slice(w * window, (w + 1) * window)
         for sub in range(subs):
             scores = mm(vk[:, cols], diagonal(qmat[:, cols], sub), 1, 1)
@@ -159,10 +183,10 @@
             )
             for j in range(receivers):
                 if slab < HD:
-                    numerator, mine = chosen[j * rows : (j + 1) * rows], stats
+                    numerator, kept = chosen[j * rows : (j + 1) * rows], stats
                 else:
                     span = slab // HD * audio
-                    numerator, mine = jnp.zeros((rows, LANES), F32), jnp.zeros((STATS, LANES), F32)
+                    numerator, kept = jnp.zeros((rows, LANES), F32), jnp.zeros((STATS, LANES), F32)
                     for i in range(LANES // span):
                         shift = (i - j) * span % LANES
                         part, part_stats = chosen[i * rows : (i + 1) * rows], stats
@@ -172,14 +196,25 @@
                         numerator = jnp.where(
                             lane_of((rows, LANES)) // span == i, part, numerator
                         )
-                        mine = jnp.where(lane_of((STATS, LANES)) // span == i, part_stats, mine)
+                        kept = jnp.where(lane_of((STATS, LANES)) // span == i, part_stats, kept)
                 target = (w * subs + sub) * receivers + j
                 p_send[target, 0:rows] = numerator.astype(BF16)
-                p_send[target, rows : rows + STATS] = mine.astype(BF16)
-
-    each_peer(lambda peer: remote(p_send.at[peer], p_recv.at[me], 2, peer).start())
+                p_send[target, rows : rows + STATS] = kept.astype(BF16)
+
+    for i in range(half):
+        index = lax.rem(chip + (i + half // 2) % half, half)
+        target = core * half + index
+
+        @pl.when(me != target)
+        def _():
+            remote(p_send.at[index], p_recv.at[chip], 2, target).start()
+
     kv_within()
-    p_recv[me] = p_send[me]
+    own_part = lax.div(me, half) == core
+
+    @pl.when(own_part)
+    def _():
+        p_recv[chip] = p_send[me - core * half]
 
     store = pltpu.make_async_copy(vmix, vmix_out, out_sem)
 
@@ -197,7 +232,14 @@
                 mixed = term if mixed is None else mixed + term
             vmix[:, cols] = mixed.astype(BF16)
 
-    all_of(p_recv, 2).wait_recv()
+    @pl.when(own_part)
+    def _():
+        all_of(p_recv, 2, half - 1).wait_recv()
+
+    @pl.when(jnp.logical_not(own_part))
+    def _():
+        all_of(p_recv, 2, half).wait_recv()
+
     loads[4].wait()
     parts = p_recv[...].astype(F32)
     peaks = parts[:, rows : rows + 1]
@@ -258,9 +300,32 @@
 
     all_of(g_kv, 1, far - 1).wait_send()
     all_of(g_kv, 6, far * (near - 1)).wait_send()
-    for phase, ref in ((0, g_q), (2, p_send), (3, a_send), (4, g_n), (5, o_send)):
+    for copy in shared:
+        copy.wait_send()
+
+    @pl.when(own_part)
+    def _():
+        all_of(p_send, 2, half - 1).wait_send()
+
+    @pl.when(jnp.logical_not(own_part))
+    def _():
+        all_of(p_send, 2, half).wait_send()
+
+    for phase, ref in ((0, g_q), (3, a_send), (4, g_n), (5, o_send)):
         all_of(ref, phase).wait_send()
     store.wait()
+
+
+def write_results(mixed, result, mixed_out, result_out, sem):
+    size = mixed.shape[0] // PIECES
+    copies = [pltpu.make_async_copy(result, result_out, sem.at[PIECES])]
+    for i in range(PIECES):
+        rows = pl.ds(i * size, size)
+        copies.append(pltpu.make_async_copy(mixed.at[rows], mixed_out.at[rows], sem.at[i]))
+    for copy in copies:
+        copy.start()
+    for copy in copies:
+        copy.wait()
 
 
 def local(n, audio_stream, audio_qkv, video_qkv, attention_out, norm_gain, weight_in, weight_out):
@@ -274,8 +339,8 @@
     vmem = pl.BlockSpec(memory_space=pltpu.VMEM)
     anywhere = pl.BlockSpec(memory_space=pltpu.HBM)
     gathered = pltpu.VMEM((n, block, LANES), BF16)
-    parts = pltpu.VMEM((n, part, LANES), BF16)
-    return pl.pallas_call(
+    parts = pltpu.VMEM((n // 2, part, LANES), BF16)
+    mixed, result = pl.pallas_call(
         functools.partial(kernel, n, math.gcd(n, NEAR)),
         out_shape=(
             jax.ShapeDtypeStruct((video, width), BF16),
@@ -288,19 +353,20 @@
             pltpu.VMEM(audio_qkv.shape, BF16),
             pltpu.VMEM((chunks, LANES), F32),
             pltpu.VMEM((video, width), BF16),
-            pltpu.VMEM((video, width), BF16),
-            pltpu.VMEM((video, width), BF16),
-            pltpu.VMEM((width, video), BF16),
+            pltpu.VMEM((2 * video, width // 2), BF16),
+            pltpu.VMEM((2 * video, width // 2), BF16),
+            pltpu.VMEM((width // 2, 2 * video), BF16),
             pltpu.VMEM(attention_out.shape, BF16),
             pltpu.VMEM(weight_in.shape, BF16),
             pltpu.VMEM(weight_out.shape, BF16),
             pltpu.VMEM((video, width), BF16),
             pltpu.VMEM((audio * chunks, LANES), F32),
             pltpu.VMEM((block, LANES), F32),
+            pltpu.VMEM((audio, width // 2), BF16),
             pltpu.VMEM((audio, width), BF16),
             pltpu.VMEM((audio, width), BF16),
-            pltpu.VMEM((audio, width), BF16),
-            gathered,
+            pltpu.VMEM((2, block // 2, LANES), BF16),
+            pltpu.VMEM((n, block // 2, LANES), BF16),
             pltpu.VMEM((n, 2 * block, LANES), BF16),
             parts,
             parts,
@@ -311,8 +377,8 @@
             gathered,
             pltpu.SemaphoreType.DMA((9,)),
             pltpu.SemaphoreType.DMA,
-            pltpu.SemaphoreType.DMA((7,)),
-            pltpu.SemaphoreType.DMA((7,)),
+            pltpu.SemaphoreType.DMA((9,)),
+            pltpu.SemaphoreType.DMA((9,)),
         ],
         compiler_params=pltpu.CompilerParams(
             collective_id=0, has_side_effects=True, vmem_limit_bytes=60 * 1024 * 1024
@@ -327,6 +393,18 @@
         weight_in,
         weight_out,
     )
+    return pl.pallas_call(
+        write_results,
+        out_shape=(
+            jax.ShapeDtypeStruct(mixed.shape, BF16),
+            jax.ShapeDtypeStruct(result.shape, BF16),
+        ),
+        in_specs=[anywhere] * 2,
+        out_specs=(anywhere, anywhere),
+        scratch_shapes=[pltpu.SemaphoreType.DMA((PIECES + 1,))],
+        compiler_params=pltpu.CompilerParams(vmem_limit_bytes=60 * 1024 * 1024),
+        name="write_results",
+    )(mixed, result)
 
 
 def solution(mesh):

time: 40.5 us -> 51.7 us (1.28)
  Pallas kernels: 36.5 us -> 50.9 us
  local copies, waits for them, and re-layouts: 3.18 us -> 0 us
    pallas_call x0 -> x1, Pallas kernels: none -> 17.3 us  [local(): pl.pallas_call(write_results, out_shape=(jax.ShapeDtypeStruct(mixed.shape...]
    unnamed x2 -> x0, local copies, waits for them, and re-layouts: 3.18 us -> none
    pallas_call x1, Pallas kernels: 36.5 us -> 33.6 us  [local(): pl.pallas_call(functools.partial(kernel, n, math.gcd(n, NEAR)), out_shape...]
where the time goes in v3:
time: 51.7 us; the launch traced here: 51.5 us
  Pallas kernels  50.9 us (98%)
  between operations  0.64 us (1%)
    pallas_call x1, Pallas kernels, local(): pl.pallas_call(functools.partial(kernel, n, math.gcd(n, NEAR)), out_shape...  33.6 us
    pallas_call x1, Pallas kernels, local(): pl.pallas_call(write_results, out_shape=(jax.ShapeDtypeStruct(mixed.shape...  17.3 us

profile of v3, /device:TPU:0, one launch (start us, length us, event | category | flops | bytes accessed | tf_op | source)
XLA Modules:
  0.0 51.5 jit_solution(8800111925968792705)
XLA Ops:
  0.6 33.6 %cross_modal_layer.1 = (bf16[128,2048]{1,0:T(8,128)(2,1)}, bf16[2,2048]{1,0:T(2,128)(2,1)}) custom-call(bf16[2,2048]{1,0:T(2,128)(2,1)} %stream_in.1, bf16[3,2,2048]{2,1,0:T(2,128)(2,1)} %aqkv_in.1, bf16[3,128,2048]{2,1,0:T(8,128)(2,1)} %vqkv.1, bf16[128,2048]{1,0:T(8,128)(2,1)} %wo.1, f32[16,128]{1,0:T(8,128)} %bitcast.1, bf16[2048,512]{1,0:T(8,128)(2,1)} %w1.1, ...), custom_call_target="tpu_custom_call" | custom-call | tf_op jit(solution)/shard_map/cross_modal_layer/pallas_call | solution.py:343
  34.3 17.3 %write_results.1 = (bf16[128,2048]{1,0:T(8,128)(2,1)}, bf16[2,2048]{1,0:T(2,128)(2,1)}) custom-call(bf16[128,2048]{1,0:T(8,128)(2,1)} %get-tuple-element.4.mixed, bf16[2,2048]{1,0:T(2,128)(2,1)} %get-tuple-element.5.result), custom_call_target="tpu_custom_call" | custom-call | tf_op jit(solution)/shard_map/write_results/pallas_call | solution.py:396

commit v4 on v3

--- a/solution.py
+++ b/solution.py
@@ -33,6 +33,7 @@
     vmix_out, result,
     stream, aqkv, gain, vq, vk, vv, vt, wo_v, w1_v, w2_v, vmix,
     relay, relay_own, qmat, kmat, vmat,
+    attended_v, x_send, x_recv, n_send,
     q_send, g_q, g_kv, p_send, p_recv, a_send, a_recv, g_n, o_send, o_recv,
     load_sem, out_sem, send_sem, recv_sem,
 ):
@@ -84,8 +85,14 @@
     keys = vqkv.shape[1]
     first, second = pl.ds(0, keys), pl.ds(keys, keys)
 
-    sources = (aqkv_in, vqkv.at[1, :, mine], vqkv.at[2, :, mine], vqkv.at[0], wo, stream_in, gain_in, w1, w2)
-    places = (aqkv, vk.at[first], vv.at[first], vq, wo_v, stream, gain, w1_v, w2_v)
+    sources = (
+        aqkv_in, vqkv.at[1, :, mine], vqkv.at[2, :, mine], vqkv.at[0], wo.at[:, mine],
+        stream_in, gain_in, w1.at[mine], w2.at[:, mine],
+    )
+    places = (
+        aqkv, vk.at[first], vv.at[first], vq, wo_v.at[core],
+        stream, gain, w1_v.at[core], w2_v.at[core],
+    )
     loads = [
         pltpu.make_async_copy(src, dst, load_sem.at[i])
         for i, (src, dst) in enumerate(zip(sources, places))
@@ -93,9 +100,13 @@
     for load in loads:
         load.start()
 
-    def own_blocks(value):
+    def own_rows(c, split):
+        step = chunks // split
+        return pl.ds(c // step * tokens * step + c % step, tokens, stride=step)
+
+    def own_blocks(value, split=1):
         for c in range(chunks):
-            relay_own[pl.ds(c, tokens, stride=chunks), :] = value[:, c * LANES : (c + 1) * LANES]
+            relay_own[own_rows(c, split), :] = value[:, c * LANES : (c + 1) * LANES]
         return relay_own[...]
 
     far = n // near
@@ -115,9 +126,8 @@
             remote(g_kv.at[kv_row], g_kv.at[kv_row], 6, peer).start()
 
     loads[0].wait()
-    queries = (own_blocks(aqkv[0].astype(F32)) * SCALE).reshape(tokens, 2, chunks // 2, LANES)
-    for h in range(2):
-        q_send[h] = queries[:, h].reshape(block // 2, LANES).astype(BF16)
+    queries = own_blocks(aqkv[0].astype(F32), 2) * SCALE
+    q_send[...] = queries.astype(BF16).reshape(q_send.shape)
     g_q[me] = q_send[core]
     g_kv[kv_slot, 0:block] = (own_blocks(aqkv[1].astype(F32)) * SCALE).astype(BF16)
     g_kv[kv_slot, block : 2 * block] = own_blocks(aqkv[2].astype(F32)).astype(BF16)
@@ -141,9 +151,10 @@
         )
 
     def blocks_of(value):
-        for c in range(chunks):
-            relay[pl.ds(c, audio, stride=chunks), :] = value[:, c * LANES : (c + 1) * LANES]
-        return relay[...].astype(BF16).reshape(n, block, LANES)
+        step = chunks // 2
+        for c in range(step):
+            relay[pl.ds(c, audio, stride=step), :] = value[:, c * LANES : (c + 1) * LANES]
+        return relay[0 : audio * step].astype(BF16).reshape(n, block // 2, LANES)
 
     def diagonal(part, sub):
         head = lane_of(part.shape) // HD
@@ -210,6 +221,13 @@
             remote(p_send.at[index], p_recv.at[chip], 2, target).start()
 
     kv_within()
+    weights_shared = [
+        remote(wo.at[:, theirs], wo_v.at[core], 9, partner),
+        remote(w1.at[theirs], w1_v.at[core], 10, partner),
+        remote(w2.at[:, theirs], w2_v.at[core], 11, partner),
+    ]
+    for copy in weights_shared:
+        copy.start()
     own_part = lax.div(me, half) == core
 
     @pl.when(own_part)
@@ -240,7 +258,6 @@
     def _():
         all_of(p_recv, 2, half).wait_recv()
 
-    loads[4].wait()
     parts = p_recv[...].astype(F32)
     peaks = parts[:, rows : rows + 1]
     scales = jnp.exp(peaks - jnp.max(peaks, axis=0, keepdims=True))
@@ -266,38 +283,64 @@
         each_peer(lambda peer: remote(send.at[peer], recv.at[me], phase, peer).start())
         recv[me] = send[me]
 
-    scatter(mm(columns, wo_v[...], 1, 0), a_send, a_recv, 3)
+    def gathered_sum(recv):
+        total = jnp.sum(recv[...].astype(F32).reshape(half, block, LANES), axis=0)
+        return total.reshape(2, tokens, chunks // 2, LANES)
+
+    attended_v[core] = columns
+    swap = remote(attended_v.at[core], attended_v.at[core], 12, partner)
+    swap.start()
+    loads[4].wait()
+    part = mm(columns, wo_v[core], 1, 0)
+    weights_shared[0].wait_recv()
+    swap.wait_recv()
+    part = part + mm(attended_v[1 - core], wo_v[1 - core], 1, 0)
+    scatter(part, a_send, a_recv, 3)
     loads[5].wait()
     loads[6].wait()
-    own = own_blocks(stream[...].astype(F32))
+    own = own_blocks(stream[...].astype(F32), 2).reshape(2, tokens, chunks // 2, LANES)
     all_of(g_kv, 6, far * (near - 1)).wait_recv()
     loads[3].wait()
     kmat[...] = rows_of(g_kv[:, 0:block])
     vmat[...] = rows_of(g_kv[:, block : 2 * block])
     video(0, windows // 2)
     all_of(a_recv, 3).wait_recv()
-    mixed_audio = own + jnp.sum(a_recv[...].astype(F32), axis=0)
-
-    by_token = mixed_audio.reshape(tokens, chunks, LANES)
-    square = jnp.sum(jnp.sum(by_token * by_token, axis=1, keepdims=True), axis=2, keepdims=True)
-    normed = by_token * lax.rsqrt(square / width + EPSILON) * gain[...][None]
-    g_n[me] = normed.reshape(block, LANES).astype(BF16)
-    each_peer(lambda peer: remote(g_n.at[me], g_n.at[me], 4, peer).start())
+    mixed_audio = own + gathered_sum(a_recv)
+
+    square = jnp.sum(mixed_audio * mixed_audio, axis=2, keepdims=True)
+    square = jnp.sum(jnp.sum(square, axis=0, keepdims=True), axis=3, keepdims=True)
+    scaled = gain[...].reshape(2, 1, chunks // 2, LANES)
+    normed = mixed_audio * lax.rsqrt(square / width + EPSILON) * scaled
+    n_send[...] = normed.reshape(2, block // 2, LANES).astype(BF16)
+    g_n[me] = n_send[core]
+    each_peer(lambda peer: remote(n_send.at[lax.rem(peer, 2)], g_n.at[me], 4, peer).start())
     video(windows // 2, windows)
     store.start()
     loads[7].wait()
     loads[8].wait()
+    weights_shared[1].wait_recv()
+    weights_shared[2].wait_recv()
     all_of(g_n, 4).wait_recv()
 
-    hidden = jax.nn.gelu(mm(rows_of(g_n[...]), w1_v[...], 1, 0), approximate=True)
-    scatter(mm(hidden.astype(BF16), w2_v[...], 1, 0), o_send, o_recv, 5)
+    features = rows_of(g_n[...])
+    for k in range(2):
+        x_send[k] = mm(features, w1_v[k], 1, 0)
+    trade = remote(x_send, x_recv, 13, partner)
+    trade.start()
+    trade.wait_recv()
+    part = None
+    for k in range(2):
+        hidden = jax.nn.gelu(x_send[k] + x_recv[k], approximate=True).astype(BF16)
+        term = mm(hidden, w2_v[k], 1, 0)
+        part = term if part is None else part + term
+    scatter(part, o_send, o_recv, 5)
     all_of(o_recv, 5).wait_recv()
-    relay_own[...] = mixed_audio + jnp.sum(o_recv[...].astype(F32), axis=0)
+    relay_own[...] = (mixed_audio + gathered_sum(o_recv)).reshape(block, LANES)
     for c in range(chunks):
-        result[:, c * LANES : (c + 1) * LANES] = relay_own[
-            pl.ds(c, tokens, stride=chunks), :
-        ].astype(BF16)
-
+        result[:, c * LANES : (c + 1) * LANES] = relay_own[own_rows(c, 2), :].astype(BF16)
+
+    for copy in weights_shared + [swap, trade]:
+        copy.wait_send()
     all_of(g_kv, 1, far - 1).wait_send()
     all_of(g_kv, 6, far * (near - 1)).wait_send()
     for copy in shared:
@@ -316,16 +359,21 @@
     store.wait()
 
 
-def write_results(mixed, result, mixed_out, result_out, sem):
+def write_results(mixed, result, mixed_out, result_out, mixed_v, result_v, sem):
     size = mixed.shape[0] // PIECES
-    copies = [pltpu.make_async_copy(result, result_out, sem.at[PIECES])]
+    moves = [(result, result_v, result_out)]
     for i in range(PIECES):
         rows = pl.ds(i * size, size)
-        copies.append(pltpu.make_async_copy(mixed.at[rows], mixed_out.at[rows], sem.at[i]))
-    for copy in copies:
-        copy.start()
-    for copy in copies:
-        copy.wait()
+        moves.append((mixed.at[rows], mixed_v.at[rows], mixed_out.at[rows]))
+    reads = [pltpu.make_async_copy(a, b, sem.at[0, i]) for i, (a, b, _) in enumerate(moves)]
+    writes = [pltpu.make_async_copy(b, c, sem.at[1, i]) for i, (_, b, c) in enumerate(moves)]
+    for read in reads:
+        read.start()
+    for read, write in zip(reads, writes):
+        read.wait()
+        write.start()
+    for write in writes:
+        write.wait()
 
 
 def local(n, audio_stream, audio_qkv, video_qkv, attention_out, norm_gain, weight_in, weight_out):
@@ -338,7 +386,8 @@
     part = HD // receivers + STATS
     vmem = pl.BlockSpec(memory_space=pltpu.VMEM)
     anywhere = pl.BlockSpec(memory_space=pltpu.HBM)
-    gathered = pltpu.VMEM((n, block, LANES), BF16)
+    hidden = weight_in.shape[1]
+    gathered = pltpu.VMEM((n, block // 2, LANES), BF16)
     parts = pltpu.VMEM((n // 2, part, LANES), BF16)
     mixed, result = pl.pallas_call(
         functools.partial(kernel, n, math.gcd(n, NEAR)),
@@ -356,15 +405,19 @@
             pltpu.VMEM((2 * video, width // 2), BF16),
             pltpu.VMEM((2 * video, width // 2), BF16),
             pltpu.VMEM((width // 2, 2 * video), BF16),
-            pltpu.VMEM(attention_out.shape, BF16),
-            pltpu.VMEM(weight_in.shape, BF16),
-            pltpu.VMEM(weight_out.shape, BF16),
+            pltpu.VMEM((2, attention_out.shape[0], width // 2), BF16),
+            pltpu.VMEM((2, width // 2, hidden), BF16),
+            pltpu.VMEM((2, hidden, width // 2), BF16),
             pltpu.VMEM((video, width), BF16),
             pltpu.VMEM((audio * chunks, LANES), F32),
             pltpu.VMEM((block, LANES), F32),
             pltpu.VMEM((audio, width // 2), BF16),
             pltpu.VMEM((audio, width), BF16),
             pltpu.VMEM((audio, width), BF16),
+            pltpu.VMEM((2, audio, attention_out.shape[0]), BF16),
+            pltpu.VMEM((2, audio, hidden), F32),
+            pltpu.VMEM((2, audio, hidden), F32),
+            pltpu.VMEM((2, block // 2, LANES), BF16),
             pltpu.VMEM((2, block // 2, LANES), BF16),
             pltpu.VMEM((n, block // 2, LANES), BF16),
             pltpu.VMEM((n, 2 * block, LANES), BF16),
@@ -377,8 +430,8 @@
             gathered,
             pltpu.SemaphoreType.DMA((9,)),
             pltpu.SemaphoreType.DMA,
-            pltpu.SemaphoreType.DMA((9,)),
-            pltpu.SemaphoreType.DMA((9,)),
+            pltpu.SemaphoreType.DMA((14,)),
+            pltpu.SemaphoreType.DMA((14,)),
         ],
         compiler_params=pltpu.CompilerParams(
             collective_id=0, has_side_effects=True, vmem_limit_bytes=60 * 1024 * 1024
@@ -401,7 +454,11 @@
         ),
         in_specs=[anywhere] * 2,
         out_specs=(anywhere, anywhere),
-        scratch_shapes=[pltpu.SemaphoreType.DMA((PIECES + 1,))],
+        scratch_shapes=[
+            pltpu.VMEM(mixed.shape, BF16),
+            pltpu.VMEM(result.shape, BF16),
+            pltpu.SemaphoreType.DMA((2, PIECES + 1)),
+        ],
         compiler_params=pltpu.CompilerParams(vmem_limit_bytes=60 * 1024 * 1024),
         name="write_results",
     )(mixed, result)

time: 51.7 us -> 35.4 us (0.68)
  Pallas kernels: 50.9 us -> 34.5 us
    pallas_call x1, Pallas kernels: 17.3 us -> 1.85 us  [local(): pl.pallas_call(write_results, out_shape=(jax.ShapeDtypeStruct(mixed.shape...]
    pallas_call x1, Pallas kernels: 33.6 us -> 32.7 us  [local(): pl.pallas_call(functools.partial(kernel, n, math.gcd(n, NEAR)), out_shape...]
where the time goes in v4:
time: 35.4 us; the launch traced here: 35.2 us
  Pallas kernels  34.5 us (97%)
  between operations  0.64 us (2%)
    pallas_call x1, Pallas kernels, local(): pl.pallas_call(functools.partial(kernel, n, math.gcd(n, NEAR)), out_shape...  32.7 us
    pallas_call x1, Pallas kernels, local(): pl.pallas_call(write_results, out_shape=(jax.ShapeDtypeStruct(mixed.shape...  1.85 us

profile of v4, /device:TPU:0, one launch (start us, length us, event | category | flops | bytes accessed | tf_op | source)
XLA Modules:
  0.0 35.2 jit_solution(17742623990409046177)
XLA Ops:
  0.6 32.7 %cross_modal_layer.1 = (bf16[128,2048]{1,0:T(8,128)(2,1)}, bf16[2,2048]{1,0:T(2,128)(2,1)}) custom-call(bf16[2,2048]{1,0:T(2,128)(2,1)} %stream_in.1, bf16[3,2,2048]{2,1,0:T(2,128)(2,1)} %aqkv_in.1, bf16[3,128,2048]{2,1,0:T(8,128)(2,1)} %vqkv.1, bf16[128,2048]{1,0:T(8,128)(2,1)} %wo.1, f32[16,128]{1,0:T(8,128)} %bitcast.1, bf16[2048,512]{1,0:T(8,128)(2,1)} %w1.1, ...), custom_call_target="tpu_custom_call" | custom-call | tf_op jit(solution)/shard_map/cross_modal_layer/pallas_call | solution.py:392
  33.3 1.9 %write_results.1 = (bf16[128,2048]{1,0:T(8,128)(2,1)}, bf16[2,2048]{1,0:T(2,128)(2,1)}) custom-call(bf16[128,2048]{1,0:T(8,128)(2,1)} %get-tuple-element.4.mixed, bf16[2,2048]{1,0:T(2,128)(2,1)} %get-tuple-element.5.result), custom_call_target="tpu_custom_call" | custom-call | tf_op jit(solution)/shard_map/write_results/pallas_call | solution.py:449

commit v5 on v4

--- a/solution.py
+++ b/solution.py
@@ -33,12 +33,12 @@
     vmix_out, result,
     stream, aqkv, gain, vq, vk, vv, vt, wo_v, w1_v, w2_v, vmix,
     relay, relay_own, qmat, kmat, vmat,
-    attended_v, x_send, x_recv, n_send,
+    attended_v, x_send, x_recv, mix_send, mix,
     q_send, g_q, g_kv, p_send, p_recv, a_send, a_recv, g_n, o_send, o_recv,
     load_sem, out_sem, send_sem, recv_sem,
 ):
     me = lax.axis_index("seq")
-    tokens, width = stream.shape
+    tokens, width = stream_in.shape
     chunks = width // LANES
     block = tokens * chunks
     audio = n * tokens
@@ -64,6 +64,11 @@
         for i in range(n - 1):
             act(lax.rem(me + 1 + (i + n // 2 - 1) % (n - 1), n))
 
+    def each_chip(act):
+        for i in range(1, n // 2):
+            other = lax.rem(chip + (i + n // 4 - 1) % (n // 2 - 1) + 1, n // 2)
+            act(other, other * 2 + core)
+
     def all_of(ref, phase, count=n - 1):
         part = ref.at[pl.ds(0, count)]
         return remote(part, part, phase, lax.rem(me + 1, n))
@@ -87,11 +92,11 @@
 
     sources = (
         aqkv_in, vqkv.at[1, :, mine], vqkv.at[2, :, mine], vqkv.at[0], wo.at[:, mine],
-        stream_in, gain_in, w1.at[mine], w2.at[:, mine],
+        stream_in.at[:, mine], gain_in, w1.at[mine], w2.at[:, mine],
     )
     places = (
         aqkv, vk.at[first], vv.at[first], vq, wo_v.at[core],
-        stream, gain, w1_v.at[core], w2_v.at[core],
+        stream.at[core], gain, w1_v.at[core], w2_v.at[core],
     )
     loads = [
         pltpu.make_async_copy(src, dst, load_sem.at[i])
@@ -222,6 +227,7 @@
 
     kv_within()
     weights_shared = [
+        remote(stream_in.at[:, theirs], stream.at[core], 14, partner),
         remote(wo.at[:, theirs], wo_v.at[core], 9, partner),
         remote(w1.at[theirs], w1_v.at[core], 10, partner),
         remote(w2.at[:, theirs], w2_v.at[core], 11, partner),
@@ -284,62 +290,83 @@
         recv[me] = send[me]
 
     def gathered_sum(recv):
-        total = jnp.sum(recv[...].astype(F32).reshape(half, block, LANES), axis=0)
-        return total.reshape(2, tokens, chunks // 2, LANES)
+        return jnp.sum(recv[...].astype(F32).reshape(half, block, LANES), axis=0)
+
+    step = chunks // 2
 
     attended_v[core] = columns
     swap = remote(attended_v.at[core], attended_v.at[core], 12, partner)
     swap.start()
     loads[4].wait()
     part = mm(columns, wo_v[core], 1, 0)
-    weights_shared[0].wait_recv()
+    weights_shared[1].wait_recv()
     swap.wait_recv()
     part = part + mm(attended_v[1 - core], wo_v[1 - core], 1, 0)
-    scatter(part, a_send, a_recv, 3)
+    a_send[...] = blocks_of(part).reshape(a_send.shape)
+    each_chip(lambda other, peer: remote(a_send.at[other], a_recv.at[chip], 3, peer).start())
+    a_recv[chip] = a_send[chip]
     loads[5].wait()
     loads[6].wait()
-    own = own_blocks(stream[...].astype(F32), 2).reshape(2, tokens, chunks // 2, LANES)
+    weights_shared[0].wait_recv()
+    for k in range(2):
+        shown = stream[k].astype(F32)
+        for c in range(step):
+            relay_own[pl.ds(k * tokens * step + c, tokens, stride=step), :] = shown[
+                :, c * LANES : (c + 1) * LANES
+            ]
+    own = relay_own[...]
     all_of(g_kv, 6, far * (near - 1)).wait_recv()
     loads[3].wait()
     kmat[...] = rows_of(g_kv[:, 0:block])
     vmat[...] = rows_of(g_kv[:, block : 2 * block])
     video(0, windows // 2)
-    all_of(a_recv, 3).wait_recv()
+    all_of(a_recv, 3, half - 1).wait_recv()
     mixed_audio = own + gathered_sum(a_recv)
 
-    square = jnp.sum(mixed_audio * mixed_audio, axis=2, keepdims=True)
-    square = jnp.sum(jnp.sum(square, axis=0, keepdims=True), axis=3, keepdims=True)
-    scaled = gain[...].reshape(2, 1, chunks // 2, LANES)
-    normed = mixed_audio * lax.rsqrt(square / width + EPSILON) * scaled
-    n_send[...] = normed.reshape(2, block // 2, LANES).astype(BF16)
-    g_n[me] = n_send[core]
-    each_peer(lambda peer: remote(n_send.at[lax.rem(peer, 2)], g_n.at[me], 4, peer).start())
+    half_gain = gain[pl.ds(pl.multiple_of(core * step, step), step), :]
+    scaled = mixed_audio.reshape(2 * tokens, step, LANES) * half_gain[None]
+    g_n[chip] = scaled.reshape(block, LANES).astype(BF16)
+    each_chip(lambda other, peer: remote(g_n.at[chip], g_n.at[chip], 4, peer).start())
+    mix_send[...] = mixed_audio.reshape(2, block // 2, LANES)
+    mix[core] = mix_send[core]
+    exchange = remote(mix_send.at[1 - core], mix.at[core], 15, partner)
+    exchange.start()
     video(windows // 2, windows)
     store.start()
     loads[7].wait()
     loads[8].wait()
-    weights_shared[1].wait_recv()
     weights_shared[2].wait_recv()
-    all_of(g_n, 4).wait_recv()
+    weights_shared[3].wait_recv()
+    all_of(g_n, 4, half - 1).wait_recv()
 
     features = rows_of(g_n[...])
+    units = w2.shape[0]
     for k in range(2):
-        x_send[k] = mm(features, w1_v[k], 1, 0)
+        x_send[k, :, 0:units] = mm(features, w1_v[k], 1, 0)
+    inverse = 1.0 / jnp.concatenate([half_gain[c : c + 1] for c in range(step)], axis=1)
+    plain = features.astype(F32) * inverse
+    square = jnp.sum(plain * plain, axis=1, keepdims=True)
+    for k in range(2):
+        x_send[k, :, units:] = jnp.broadcast_to(square, (audio, LANES))
     trade = remote(x_send, x_recv, 13, partner)
     trade.start()
     trade.wait_recv()
+    square = (x_send[0, :, units:] + x_recv[0, :, units:])[:, 0:1]
+    factor = lax.rsqrt(square / width + EPSILON)
     part = None
     for k in range(2):
-        hidden = jax.nn.gelu(x_send[k] + x_recv[k], approximate=True).astype(BF16)
+        total = x_send[k, :, 0:units] + x_recv[k, :, 0:units]
+        hidden = jax.nn.gelu(total * factor, approximate=True).astype(BF16)
         term = mm(hidden, w2_v[k], 1, 0)
         part = term if part is None else part + term
     scatter(part, o_send, o_recv, 5)
     all_of(o_recv, 5).wait_recv()
-    relay_own[...] = (mixed_audio + gathered_sum(o_recv)).reshape(block, LANES)
+    exchange.wait_recv()
+    relay_own[...] = mix[...].reshape(block, LANES) + gathered_sum(o_recv)
     for c in range(chunks):
         result[:, c * LANES : (c + 1) * LANES] = relay_own[own_rows(c, 2), :].astype(BF16)
 
-    for copy in weights_shared + [swap, trade]:
+    for copy in weights_shared + [swap, trade, exchange]:
         copy.wait_send()
     all_of(g_kv, 1, far - 1).wait_send()
     all_of(g_kv, 6, far * (near - 1)).wait_send()
@@ -354,7 +381,9 @@
     def _():
         all_of(p_send, 2, half).wait_send()
 
-    for phase, ref in ((0, g_q), (3, a_send), (4, g_n), (5, o_send)):
+    for phase, ref in ((3, a_send), (4, g_n)):
+        all_of(ref, phase, half - 1).wait_send()
+    for phase, ref in ((0, g_q), (5, o_send)):
         all_of(ref, phase).wait_send()
     store.wait()
 
@@ -388,6 +417,7 @@
     anywhere = pl.BlockSpec(memory_space=pltpu.HBM)
     hidden = weight_in.shape[1]
     gathered = pltpu.VMEM((n, block // 2, LANES), BF16)
+    by_chip = pltpu.VMEM((n // 2, block, LANES), BF16)
     parts = pltpu.VMEM((n // 2, part, LANES), BF16)
     mixed, result = pl.pallas_call(
         functools.partial(kernel, n, math.gcd(n, NEAR)),
@@ -398,7 +428,7 @@
         in_specs=[anywhere] * 7,
         out_specs=(anywhere, vmem),
         scratch_shapes=[
-            pltpu.VMEM(audio_stream.shape, BF16),
+            pltpu.VMEM((2, tokens, width // 2), BF16),
             pltpu.VMEM(audio_qkv.shape, BF16),
             pltpu.VMEM((chunks, LANES), F32),
             pltpu.VMEM((video, width), BF16),
@@ -415,23 +445,24 @@
             pltpu.VMEM((audio, width), BF16),
             pltpu.VMEM((audio, width), BF16),
             pltpu.VMEM((2, audio, attention_out.shape[0]), BF16),
-            pltpu.VMEM((2, audio, hidden), F32),
-            pltpu.VMEM((2, audio, hidden), F32),
-            pltpu.VMEM((2, block // 2, LANES), BF16),
+            pltpu.VMEM((2, audio, hidden + LANES), F32),
+            pltpu.VMEM((2, audio, hidden + LANES), F32),
+            pltpu.VMEM((2, block // 2, LANES), F32),
+            pltpu.VMEM((2, block // 2, LANES), F32),
             pltpu.VMEM((2, block // 2, LANES), BF16),
             pltpu.VMEM((n, block // 2, LANES), BF16),
             pltpu.VMEM((n, 2 * block, LANES), BF16),
             parts,
             parts,
-            gathered,
-            gathered,
-            gathered,
+            by_chip,
+            by_chip,
+            by_chip,
             gathered,
             gathered,
             pltpu.SemaphoreType.DMA((9,)),
             pltpu.SemaphoreType.DMA,
-            pltpu.SemaphoreType.DMA((14,)),
-            pltpu.SemaphoreType.DMA((14,)),
+            pltpu.SemaphoreType.DMA((16,)),
+            pltpu.SemaphoreType.DMA((16,)),
         ],
         compiler_params=pltpu.CompilerParams(
             collective_id=0, has_side_effects=True, vmem_limit_bytes=60 * 1024 * 1024

time: 35.4 us -> 34.8 us (0.983)
  Pallas kernels: 34.5 us -> 33.9 us
    pallas_call x1, Pallas kernels: 32.7 us -> 32.1 us  [local(): pl.pallas_call(functools.partial(kernel, n, math.gcd(n, NEAR)), out_shape...]
where the time goes in v5:
time: 34.8 us; the launch traced here: 34.6 us
  Pallas kernels  33.9 us (97%)
  between operations  0.64 us (2%)
    pallas_call x1, Pallas kernels, local(): pl.pallas_call(functools.partial(kernel, n, math.gcd(n, NEAR)), out_shape...  32.1 us
    pallas_call x1, Pallas kernels, local(): pl.pallas_call(write_results, out_shape=(jax.ShapeDtypeStruct(mixed.shape...  1.85 us

profile of v5, /device:TPU:0, one launch (start us, length us, event | category | flops | bytes accessed | tf_op | source)
XLA Modules:
  0.0 34.6 jit_solution(12512390872090536524)
XLA Ops:
  0.6 32.1 %cross_modal_layer.1 = (bf16[128,2048]{1,0:T(8,128)(2,1)}, bf16[2,2048]{1,0:T(2,128)(2,1)}) custom-call(bf16[2,2048]{1,0:T(2,128)(2,1)} %stream_in.1, bf16[3,2,2048]{2,1,0:T(2,128)(2,1)} %aqkv_in.1, bf16[3,128,2048]{2,1,0:T(8,128)(2,1)} %vqkv.1, bf16[128,2048]{1,0:T(8,128)(2,1)} %wo.1, f32[16,128]{1,0:T(8,128)} %bitcast.1, bf16[2048,512]{1,0:T(8,128)(2,1)} %w1.1, ...), custom_call_target="tpu_custom_call" | custom-call | tf_op jit(solution)/shard_map/cross_modal_layer/pallas_call | solution.py:422
  32.7 1.9 %write_results.1 = (bf16[128,2048]{1,0:T(8,128)(2,1)}, bf16[2,2048]{1,0:T(2,128)(2,1)}) custom-call(bf16[128,2048]{1,0:T(8,128)(2,1)} %get-tuple-element.4.mixed, bf16[2,2048]{1,0:T(2,128)(2,1)} %get-tuple-element.5.result), custom_call_target="tpu_custom_call" | custom-call | tf_op jit(solution)/shard_map/write_results/pallas_call | solution.py:480

commit v6 on v2

v6 whole, which is shorter than its diff:
```python
import functools
import math

import jax
import jax.numpy as jnp
from jax import lax
from jax.experimental import pallas as pl
from jax.experimental.pallas import tpu as pltpu
from jax.sharding import PartitionSpec as P

HEADS = 32
HD = 64
LANES = 128
STATS = 16
NEAR = 4
PIECES = 4
EPSILON = 1e-06
SCALE = 1.0 / math.sqrt(HD)
F32 = jnp.float32
BF16 = jnp.bfloat16


def mm(a, b, ca, cb):
    return lax.dot_general(a, b, (((ca,), (cb,)), ((), ())), preferred_element_type=F32)


def lane_of(shape):
    return lax.broadcasted_iota(jnp.int32, shape, len(shape) - 1)


def kernel(
    n, near, stream_in, aqkv_in, vqkv, wo, gain_in, w1, w2,
    vmix_out, result,
    stream, aqkv, gain, vq, vk, vv, vt, wo_v, w1_v, w2_v, vmix,
    relay, relay_own, qmat, kmat, vmat,
    g_q, g_kv, p_send, p_recv, a_send, a_recv, g_n, o_send, o_recv,
    load_sem, out_sem, send_sem, recv_sem,
):
    me = lax.axis_index("seq")
    core, chip = lax.rem(me, 2), lax.div(me, 2)
    partner = me + 1 - 2 * core
    half = n // 2
    tokens, width = stream_in.shape
    chunks = width // LANES
    block = tokens * chunks
    keys = vqkv.shape[1]
    units = w2.shape[0]
    slab = 2 * wo.shape[0]
    audio = n * tokens
    asked = half * tokens

    def remote(src, dst, phase, peer):
        return pltpu.make_async_remote_copy(
            src_ref=src,
            dst_ref=dst,
            send_sem=send_sem.at[phase],
            recv_sem=recv_sem.at[phase],
            device_id={"seq": peer},
            device_id_type=pl.DeviceIdType.MESH,
        )

    def each_chip(act):
        for i in range(1, half):
            other = lax.rem(chip + (i + half // 2 - 1) % (half - 1) + 1, half)
            act(other, other * 2 + core)

    def all_of(ref, phase, count=half - 1):
        part = ref.at[pl.ds(0, count)]
        return remote(part, part, phase, partner)

    barrier = pltpu.get_barrier_semaphore()
    for i in range(1, n):
        pl.semaphore_signal(
            barrier,
            inc=1,
            device_id={"seq": lax.rem(me + i, n)},
            device_id_type=pl.DeviceIdType.MESH,
        )

    first, second = pl.ds(0, keys), pl.ds(keys, keys)
    wo_rows = pl.ds(pl.multiple_of(core * (slab // 2), slab // 2), slab // 2)
    sources = (aqkv_in, vqkv.at[1], vqkv.at[2], vqkv.at[0], wo, stream_in, gain_in, w1, w2)
    places = (
        aqkv, vk.at[first], vv.at[first], vq, wo_v.at[wo_rows],
        stream, gain, w1_v.at[core], w2_v.at[core],
    )
    loads = [
        pltpu.make_async_copy(src, dst, load_sem.at[i])
        for i, (src, dst) in enumerate(zip(sources, places))
    ]
    for load in loads:
        load.start()

    def own_blocks(value):
        for c in range(chunks):
            relay_own[pl.ds(c, tokens, stride=chunks), :] = value[:, c * LANES : (c + 1) * LANES]
        return relay_own[...]

    far = n // near
    my_far, my_near = lax.div(me, near), lax.rem(me, near)
    kv_slot = my_near * far + my_far
    kv_row = pl.ds(my_near * far, far)

    loads[0].wait()
    g_q[chip] = (own_blocks(aqkv[0].astype(F32)) * SCALE).astype(BF16)
    g_kv[kv_slot, 0:block] = (own_blocks(aqkv[1].astype(F32)) * SCALE).astype(BF16)
    g_kv[kv_slot, block : 2 * block] = own_blocks(aqkv[2].astype(F32)).astype(BF16)

    pl.semaphore_wait(barrier, n - 1)
    shared = [
        remote(vqkv.at[1], vk.at[second], 7, partner),
        remote(vqkv.at[2], vv.at[second], 8, partner),
        remote(wo, wo_v.at[wo_rows], 9, partner),
        remote(w1, w1_v.at[core], 10, partner),
        remote(w2, w2_v.at[core], 11, partner),
    ]
    for copy in shared[0:2]:
        copy.start()
    each_chip(lambda other, peer: remote(g_q.at[chip], g_q.at[chip], 0, peer).start())
    for i in range(1, far):
        peer = lax.rem(my_far + i, far) * near + my_near
        remote(g_kv.at[kv_slot], g_kv.at[kv_slot], 1, peer).start()

    def rows_of(blocks):
        step = chunks
        count = blocks.shape[0] * blocks.shape[1]
        relay[0:count] = blocks.astype(F32).reshape(count, LANES)
        return jnp.concatenate(
            [
                relay[pl.ds(c, count // step, stride=step), :].astype(BF16)
                for c in range(step)
            ],
            axis=1,
        )

    def blocks_of(value):
        for c in range(chunks):
            relay[pl.ds(c, asked, stride=chunks), :] = value[:, c * LANES : (c + 1) * LANES]
        return relay[0 : asked * chunks].astype(BF16).reshape(half, block, LANES)

    def scatter(value, send, recv, phase):
        send[...] = blocks_of(value)
        each_chip(lambda other, peer: remote(send.at[other], recv.at[chip], phase, peer).start())
        recv[chip] = send[chip]

    def gathered_sum(recv):
        return jnp.sum(recv[...].astype(F32), axis=0)

    def diagonal(part, sub, group):
        head = lane_of(part.shape) // HD
        return jnp.concatenate(
            [jnp.where(head == sub * group + h, part, jnp.zeros_like(part)) for h in range(group)],
            axis=0,
        )

    def windows_of(rows):
        group = LANES // rows
        window = max(group * HD, LANES)
        return group, window, width // window, window // (group * HD)

    group, window, windows, subs = windows_of(asked)
    receivers = half // (windows * subs)
    rows = HD // receivers

    loads[1].wait()
    loads[2].wait()
    for copy in shared[0:2]:
        copy.wait_recv()
    for w in range(windows):
        cols = slice(w * window, (w + 1) * window)
        vt[cols, :] = vv[:, cols].T

    all_of(g_q, 0).wait_recv()
    qmat[...] = rows_of(g_q[...])

    for w in range(windows):
        cols = slice(w * window, (w + 1) * window)
        for sub in range(subs):
            scores = mm(vk[:, cols], diagonal(qmat[:, cols], sub, group), 1, 1)
            peak = jnp.max(scores, axis=0, keepdims=True).astype(BF16).astype(F32)
            weights = jnp.exp(scores - peak)
            total = jnp.sum(weights, axis=0, keepdims=True)
            product = mm(vt[cols, :], weights.astype(BF16), 1, 0)
            lane = lane_of((HD, LANES)) // asked
            chosen = jnp.zeros((HD, LANES), F32)
            for h in range(group):
                at = (sub * group + h) * HD
                chosen = jnp.where(lane == h, product[at : at + HD], chosen)
            high = total.astype(BF16).astype(F32)
            row = lax.broadcasted_iota(jnp.int32, (STATS, LANES), 0)
            stats = jnp.where(
                row == 0, peak, jnp.where(row == 1, high, jnp.where(row == 2, total - high, 0.0))
            )
            for j in range(receivers):
                if slab < HD:
                    numerator, kept = chosen[j * rows : (j + 1) * rows], stats
                else:
                    span = slab // HD * asked
                    numerator, kept = jnp.zeros((rows, LANES), F32), jnp.zeros((STATS, LANES), F32)
                    for i in range(LANES // span):
                        shift = (i - j) * span % LANES
                        part, part_stats = chosen[i * rows : (i + 1) * rows], stats
                        if shift:
                            part = pltpu.roll(part, shift, 1)
                            part_stats = pltpu.roll(part_stats, shift, 1)
                        numerator = jnp.where(
                            lane_of((rows, LANES)) // span == i, part, numerator
                        )
                        kept = jnp.where(lane_of((STATS, LANES)) // span == i, part_stats, kept)
                target = (w * subs + sub) * receivers + j
                p_send[target, 0:rows] = numerator.astype(BF16)
                p_send[target, rows : rows + STATS] = kept.astype(BF16)

    each_chip(lambda other, peer: remote(p_send.at[other], p_recv.at[chip], 2, peer).start())
    all_of(g_kv, 1, far - 1).wait_recv()
    for i in range(1, near):
        peer = my_far * near + lax.rem(my_near + i, near)
        remote(g_kv.at[kv_row], g_kv.at[kv_row], 6, peer).start()
    for copy in shared[2:]:
        copy.start()
    p_recv[chip] = p_send[chip]

    store = pltpu.make_async_copy(vmix, vmix_out, out_sem)
    v_group, v_window, v_windows, v_subs = windows_of(audio)

    def video(start, stop):
        for w in range(start, stop):
            cols = slice(w * v_window, (w + 1) * v_window)
            mixed = None
            for sub in range(v_subs):
                scores = mm(diagonal(kmat[:, cols], sub, v_group), vq[:, cols], 1, 1)
                scores = scores.reshape(v_group, audio, scores.shape[1])
                weights = jnp.exp(scores - jnp.max(scores, axis=1, keepdims=True))
                weights = weights * (1.0 / jnp.sum(weights, axis=1, keepdims=True))
                weights = weights.reshape(v_group * audio, scores.shape[2])
                term = mm(weights.T.astype(BF16), diagonal(vmat[:, cols], sub, v_group), 1, 0)
                mixed = term if mixed is None else mixed + term
            vmix[:, cols] = mixed.astype(BF16)

    all_of(p_recv, 2).wait_recv()
    parts = p_recv[...].astype(F32)
    peaks = parts[:, rows : rows + 1]
    scales = jnp.exp(peaks - jnp.max(peaks, axis=0, keepdims=True))
    totals = (parts[:, rows + 1 : rows + 2] + parts[:, rows + 2 : rows + 3]) * scales
    attended = jnp.sum(parts[:, 0:rows] * scales, axis=0) / jnp.sum(totals, axis=0)
    turned = attended.T.astype(BF16)
    if slab < HD:
        columns = turned
    else:
        heads = slab // HD
        folds = HD // rows
        columns = jnp.concatenate(
            [
                turned[(f * heads + h) * asked : (f * heads + h + 1) * asked]
                for h in range(heads)
                for f in range(folds)
            ],
            axis=1,
        )

    loads[4].wait()
    shared[2].wait_recv()
    scatter(mm(columns, wo_v[...], 1, 0), a_send, a_recv, 3)
    loads[5].wait()
    loads[6].wait()
    own = own_blocks(stream[...].astype(F32))
    all_of(g_kv, 6, far * (near - 1)).wait_recv()
    loads[3].wait()
    kmat[...] = rows_of(g_kv[:, 0:block])
    vmat[...] = rows_of(g_kv[:, block : 2 * block])
    video(0, v_windows // 2)
    all_of(a_recv, 3).wait_recv()
    mixed_audio = own + gathered_sum(a_recv)

    by_token = mixed_audio.reshape(tokens, chunks, LANES)
    square = jnp.sum(jnp.sum(by_token * by_token, axis=1, keepdims=True), axis=2, keepdims=True)
    normed = by_token * lax.rsqrt(square / width + EPSILON) * gain[...][None]
    g_n[chip] = normed.reshape(block, LANES).astype(BF16)
    each_chip(lambda other, peer: remote(g_n.at[chip], g_n.at[chip], 4, peer).start())
    video(v_windows // 2, v_windows)
    store.start()
    loads[7].wait()
    loads[8].wait()
    shared[3].wait_recv()
    shared[4].wait_recv()
    all_of(g_n, 4).wait_recv()

    features = rows_of(g_n[...])
    part = None
    for k in range(2):
        hidden = jax.nn.gelu(mm(features, w1_v[k], 1, 0), approximate=True).astype(BF16)
        term = mm(hidden, w2_v[k], 1, 0)
        part = term if part is None else part + term
    scatter(part, o_send, o_recv, 5)
    all_of(o_recv, 5).wait_recv()
    relay_own[...] = mixed_audio + gathered_sum(o_recv)
    for c in range(chunks):
        result[:, c * LANES : (c + 1) * LANES] = relay_own[
            pl.ds(c, tokens, stride=chunks), :
        ].astype(BF16)

    for copy in shared:
        copy.wait_send()
    all_of(g_kv, 1, far - 1).wait_send()
    all_of(g_kv, 6, far * (near - 1)).wait_send()
    for phase, ref in ((0, g_q), (2, p_send), (3, a_send), (4, g_n), (5, o_send)):
        all_of(ref, phase).wait_send()
    store.wait()


def write_results(mixed, result, mixed_out, result_out, mixed_v, result_v, sem):
    size = mixed.shape[0] // PIECES
    moves = [(result, result_v, result_out)]
    for i in range(PIECES):
        rows = pl.ds(i * size, size)
        moves.append((mixed.at[rows], mixed_v.at[rows], mixed_out.at[rows]))
    reads = [pltpu.make_async_copy(a, b, sem.at[0, i]) for i, (a, b, _) in enumerate(moves)]
    writes = [pltpu.make_async_copy(b, c, sem.at[1, i]) for i, (_, b, c) in enumerate(moves)]
    for read in reads:
        read.start()
    for read, write in zip(reads, writes):
        read.wait()
        write.start()
    for write in writes:
        write.wait()


def local(n, audio_stream, audio_qkv, video_qkv, attention_out, norm_gain, weight_in, weight_out):
    tokens, width = audio_stream.shape
    chunks = width // LANES
    block = tokens * chunks
    audio = n * tokens
    video = video_qkv.shape[1]
    asked = audio // 2
    receivers = n // 2 * LANES // (asked * HEADS)
    part = HD // receivers + STATS
    hidden = weight_in.shape[1]
    slab = attention_out.shape[0]
    anywhere = pl.BlockSpec(memory_space=pltpu.HBM)
    vmem = pl.BlockSpec(memory_space=pltpu.VMEM)
    by_chip = pltpu.VMEM((n // 2, block, LANES), BF16)
    parts = pltpu.VMEM((n // 2, part, LANES), BF16)
    mixed, result = pl.pallas_call(
        functools.partial(kernel, n, math.gcd(n, NEAR)),
        out_shape=(
            jax.ShapeDtypeStruct((video, width), BF16),
            jax.ShapeDtypeStruct((tokens, width), BF16),
        ),
        in_specs=[anywhere] * 7,
        out_specs=(anywhere, vmem),
        scratch_shapes=[
            pltpu.VMEM(audio_stream.shape, BF16),
            pltpu.VMEM(audio_qkv.shape, BF16),
            pltpu.VMEM((chunks, LANES), F32),
            pltpu.VMEM((video, width), BF16),
            pltpu.VMEM((2 * video, width), BF16),
            pltpu.VMEM((2 * video, width), BF16),
            pltpu.VMEM((width, 2 * video), BF16),
            pltpu.VMEM((2 * slab, width), BF16),
            pltpu.VMEM((2, width, hidden), BF16),
            pltpu.VMEM((2, hidden, width), BF16),
            pltpu.VMEM((video, width), BF16),
            pltpu.VMEM((audio * chunks, LANES), F32),
            pltpu.VMEM((block, LANES), F32),
            pltpu.VMEM((asked, width), BF16),
            pltpu.VMEM((audio, width), BF16),
            pltpu.VMEM((audio, width), BF16),
            by_chip,
            pltpu.VMEM((n, 2 * block, LANES), BF16),
            parts,
            parts,
            by_chip,
            by_chip,
            by_chip,
            by_chip,
            by_chip,
            pltpu.SemaphoreType.DMA((9,)),
            pltpu.SemaphoreType.DMA,
            pltpu.SemaphoreType.DMA((12,)),
            pltpu.SemaphoreType.DMA((12,)),
        ],
        compiler_params=pltpu.CompilerParams(
            collective_id=0, has_side_effects=True, vmem_limit_bytes=60 * 1024 * 1024
        ),
        name="cross_modal_layer",
    )(
        audio_stream,
        audio_qkv,
        video_qkv,
        attention_out,
        norm_gain.reshape(chunks, LANES),
        weight_in,
        weight_out,
    )
    return pl.pallas_call(
        write_results,
        out_shape=(
            jax.ShapeDtypeStruct(mixed.shape, BF16),
            jax.ShapeDtypeStruct(result.shape, BF16),
        ),
        in_specs=[anywhere] * 2,
        out_specs=(anywhere, anywhere),
        scratch_shapes=[
            pltpu.VMEM(mixed.shape, BF16),
            pltpu.VMEM(result.shape, BF16),
            pltpu.SemaphoreType.DMA((2, PIECES + 1)),
        ],
        compiler_params=pltpu.CompilerParams(vmem_limit_bytes=60 * 1024 * 1024),
        name="write_results",
    )(mixed, result)


def solution(mesh):
    placed = (
        P(("groups", "seq"), None),
        P(None, ("groups", "seq"), None),
        P(None, ("groups", "seq"), None),
        P("seq", None),
        P(),
        P(None, "seq"),
        P("seq", None),
    )
    return jax.shard_map(
        functools.partial(local, mesh.shape["seq"]),
        mesh=mesh,
        in_specs=placed,
        out_specs=(P(("groups", "seq"), None), P(("groups", "seq"), None)),
        check_vma=False,
    )
```

time: 40.5 us -> 33.6 us (0.83)
  Pallas kernels: 36.5 us -> 32.7 us
  local copies, waits for them, and re-layouts: 3.18 us -> 0 us
    pallas_call x1, Pallas kernels: 36.5 us -> 30.8 us  [local(): pl.pallas_call(functools.partial(kernel, n, math.gcd(n, NEAR)), out_shape...]
    unnamed x2 -> x0, local copies, waits for them, and re-layouts: 3.18 us -> none
    pallas_call x0 -> x1, Pallas kernels: none -> 1.85 us  [local(): pl.pallas_call(write_results, out_shape=(jax.ShapeDtypeStruct(mixed.shape...]
where the time goes in v6:
time: 33.6 us; the launch traced here: 33.3 us
  Pallas kernels  32.7 us (97%)
  between operations  0.64 us (2%)
    pallas_call x1, Pallas kernels, local(): pl.pallas_call(functools.partial(kernel, n, math.gcd(n, NEAR)), out_shape...  30.8 us
    pallas_call x1, Pallas kernels, local(): pl.pallas_call(write_results, out_shape=(jax.ShapeDtypeStruct(mixed.shape...  1.85 us

profile of v6, /device:TPU:0, one launch (start us, length us, event | category | flops | bytes accessed | tf_op | source)
XLA Modules:
  0.0 33.3 jit_solution(11138123741378951529)
XLA Ops:
  0.6 30.8 %cross_modal_layer.1 = (bf16[128,2048]{1,0:T(8,128)(2,1)}, bf16[2,2048]{1,0:T(2,128)(2,1)}) custom-call(bf16[2,2048]{1,0:T(2,128)(2,1)} %stream_in.1, bf16[3,2,2048]{2,1,0:T(2,128)(2,1)} %aqkv_in.1, bf16[3,128,2048]{2,1,0:T(8,128)(2,1)} %vqkv.1, bf16[128,2048]{1,0:T(8,128)(2,1)} %wo.1, f32[16,128]{1,0:T(8,128)} %bitcast.1, bf16[2048,512]{1,0:T(8,128)(2,1)} %w1.1, ...), custom_call_target="tpu_custom_call" | custom-call | tf_op jit(solution)/shard_map/cross_modal_layer/pallas_call | solution.py:343
  31.5 1.9 %write_results.1 = (bf16[128,2048]{1,0:T(8,128)(2,1)}, bf16[2,2048]{1,0:T(2,128)(2,1)}) custom-call(bf16[128,2048]{1,0:T(8,128)(2,1)} %get-tuple-element.4.mixed, bf16[2,2048]{1,0:T(2,128)(2,1)} %get-tuple-element.5.result), custom_call_target="tpu_custom_call" | custom-call | tf_op jit(solution)/shard_map/write_results/pallas_call | solution.py:395

commit v7 on v6

--- a/solution.py
+++ b/solution.py
@@ -166,6 +166,8 @@
     loads[2].wait()
     for copy in shared[0:2]:
         copy.wait_recv()
+    for copy in shared[2:]:
+        copy.start()
     for w in range(windows):
         cols = slice(w * window, (w + 1) * window)
         vt[cols, :] = vv[:, cols].T
@@ -216,8 +218,6 @@
     for i in range(1, near):
         peer = my_far * near + lax.rem(my_near + i, near)
         remote(g_kv.at[kv_row], g_kv.at[kv_row], 6, peer).start()
-    for copy in shared[2:]:
-        copy.start()
     p_recv[chip] = p_send[chip]
 
     store = pltpu.make_async_copy(vmix, vmix_out, out_sem)
@@ -281,16 +281,18 @@
     store.start()
     loads[7].wait()
     loads[8].wait()
-    shared[3].wait_recv()
+    all_of(g_n, 4).wait_recv()
+
+    features = rows_of(g_n[...])
+    hidden = []
+    for k in range(2):
+        if k:
+            shared[3].wait_recv()
+        opened = mm(features, w1_v[core if k == 0 else 1 - core], 1, 0)
+        hidden.append(jax.nn.gelu(opened, approximate=True).astype(BF16))
+    part = mm(hidden[0], w2_v[core], 1, 0)
     shared[4].wait_recv()
-    all_of(g_n, 4).wait_recv()
-
-    features = rows_of(g_n[...])
-    part = None
-    for k in range(2):
-        hidden = jax.nn.gelu(mm(features, w1_v[k], 1, 0), approximate=True).astype(BF16)
-        term = mm(hidden, w2_v[k], 1, 0)
-        part = term if part is None else part + term
+    part = part + mm(hidden[1], w2_v[1 - core], 1, 0)
     scatter(part, o_send, o_recv, 5)
     all_of(o_recv, 5).wait_recv()
     relay_own[...] = mixed_audio + gathered_sum(o_recv)

time: 33.6 us -> 33.8 us (level)
  no operation moved by 1% of the time
where the time goes in v7:
time: 33.8 us; the launch traced here: 33.6 us
  Pallas kernels  33 us (98%)
  between operations  0.64 us (2%)
    pallas_call x1, Pallas kernels, local(): pl.pallas_call(functools.partial(kernel, n, math.gcd(n, NEAR)), out_shape...  31.1 us
    pallas_call x1, Pallas kernels, local(): pl.pallas_call(write_results, out_shape=(jax.ShapeDtypeStruct(mixed.shape...  1.85 us

profile of v7, /device:TPU:0, one launch (start us, length us, event | category | flops | bytes accessed | tf_op | source)
XLA Modules:
  0.0 33.6 jit_solution(8804720038501202260)
XLA Ops:
  0.6 31.1 %cross_modal_layer.1 = (bf16[128,2048]{1,0:T(8,128)(2,1)}, bf16[2,2048]{1,0:T(2,128)(2,1)}) custom-call(bf16[2,2048]{1,0:T(2,128)(2,1)} %stream_in.1, bf16[3,2,2048]{2,1,0:T(2,128)(2,1)} %aqkv_in.1, bf16[3,128,2048]{2,1,0:T(8,128)(2,1)} %vqkv.1, bf16[128,2048]{1,0:T(8,128)(2,1)} %wo.1, f32[16,128]{1,0:T(8,128)} %bitcast.1, bf16[2048,512]{1,0:T(8,128)(2,1)} %w1.1, ...), custom_call_target="tpu_custom_call" | custom-call | tf_op jit(solution)/shard_map/cross_modal_layer/pallas_call | solution.py:345
  31.8 1.9 %write_results.1 = (bf16[128,2048]{1,0:T(8,128)(2,1)}, bf16[2,2048]{1,0:T(2,128)(2,1)}) custom-call(bf16[128,2048]{1,0:T(8,128)(2,1)} %get-tuple-element.4.mixed, bf16[2,2048]{1,0:T(2,128)(2,1)} %get-tuple-element.5.result), custom_call_target="tpu_custom_call" | custom-call | tf_op jit(solution)/shard_map/write_results/pallas_call | solution.py:397

commit v8 on v6

--- a/solution.py
+++ b/solution.py
@@ -32,7 +32,7 @@
     n, near, stream_in, aqkv_in, vqkv, wo, gain_in, w1, w2,
     vmix_out, result,
     stream, aqkv, gain, vq, vk, vv, vt, wo_v, w1_v, w2_v, vmix,
-    relay, relay_own, qmat, kmat, vmat,
+    relay, relay_own, qmat, kmat, vmat, logits, rounded,
     g_q, g_kv, p_send, p_recv, a_send, a_recv, g_n, o_send, o_recv,
     load_sem, out_sem, send_sem, recv_sem,
 ):
@@ -114,9 +114,9 @@
         remote(w1, w1_v.at[core], 10, partner),
         remote(w2, w2_v.at[core], 11, partner),
     ]
+    each_chip(lambda other, peer: remote(g_q.at[chip], g_q.at[chip], 0, peer).start())
     for copy in shared[0:2]:
         copy.start()
-    each_chip(lambda other, peer: remote(g_q.at[chip], g_q.at[chip], 0, peer).start())
     for i in range(1, far):
         peer = lax.rem(my_far + i, far) * near + my_near
         remote(g_kv.at[kv_slot], g_kv.at[kv_slot], 1, peer).start()
@@ -164,23 +164,40 @@
 
     loads[1].wait()
     loads[2].wait()
-    for copy in shared[0:2]:
-        copy.wait_recv()
-    for w in range(windows):
-        cols = slice(w * window, (w + 1) * window)
-        vt[cols, :] = vv[:, cols].T
-
+    def turn_values(part):
+        for w in range(windows):
+            cols = slice(w * window, (w + 1) * window)
+            vt[cols, part] = vv[part, cols].T
+
+    def score(part):
+        for w in range(windows):
+            cols = slice(w * window, (w + 1) * window)
+            for sub in range(subs):
+                spread = diagonal(qmat[:, cols], sub, group)
+                logits[w * subs + sub, part] = mm(vk[part, cols], spread, 1, 1)
+
+    own_part, other_part = slice(0, keys), slice(keys, 2 * keys)
+    turn_values(own_part)
     all_of(g_q, 0).wait_recv()
     qmat[...] = rows_of(g_q[...])
+    score(own_part)
+    shared[0].wait_recv()
+    score(other_part)
+    statistics = []
+    for at in range(windows * subs):
+        scores = logits[at]
+        peak = jnp.max(scores, axis=0, keepdims=True).astype(BF16).astype(F32)
+        weights = jnp.exp(scores - peak)
+        statistics.append((peak, jnp.sum(weights, axis=0, keepdims=True)))
+        rounded[at] = weights.astype(BF16)
+    shared[1].wait_recv()
+    turn_values(other_part)
 
     for w in range(windows):
         cols = slice(w * window, (w + 1) * window)
         for sub in range(subs):
-            scores = mm(vk[:, cols], diagonal(qmat[:, cols], sub, group), 1, 1)
-            peak = jnp.max(scores, axis=0, keepdims=True).astype(BF16).astype(F32)
-            weights = jnp.exp(scores - peak)
-            total = jnp.sum(weights, axis=0, keepdims=True)
-            product = mm(vt[cols, :], weights.astype(BF16), 1, 0)
+            peak, total = statistics[w * subs + sub]
+            product = mm(vt[cols, :], rounded[w * subs + sub], 1, 0)
             lane = lane_of((HD, LANES)) // asked
             chosen = jnp.zeros((HD, LANES), F32)
             for h in range(group):
@@ -365,6 +382,8 @@
             pltpu.VMEM((asked, width), BF16),
             pltpu.VMEM((audio, width), BF16),
             pltpu.VMEM((audio, width), BF16),
+            pltpu.VMEM((HEADS * asked // LANES, 2 * video, LANES), F32),
+            pltpu.VMEM((HEADS * asked // LANES, 2 * video, LANES), BF16),
             by_chip,
             pltpu.VMEM((n, 2 * block, LANES), BF16),
             parts,

time: 33.6 us -> 33.7 us (level)
  no operation moved by 1% of the time
where the time goes in v8:
time: 33.7 us; the launch traced here: 33.5 us
  Pallas kernels  32.8 us (97%)
  between operations  0.64 us (2%)
    pallas_call x1, Pallas kernels, local(): pl.pallas_call(functools.partial(kernel, n, math.gcd(n, NEAR)), out_shape...  31 us
    pallas_call x1, Pallas kernels, local(): pl.pallas_call(write_results, out_shape=(jax.ShapeDtypeStruct(mixed.shape...  1.85 us

profile of v8, /device:TPU:0, one launch (start us, length us, event | category | flops | bytes accessed | tf_op | source)
XLA Modules:
  0.0 33.5 jit_solution(9741933797820238962)
XLA Ops:
  0.6 31.0 %cross_modal_layer.1 = (bf16[128,2048]{1,0:T(8,128)(2,1)}, bf16[2,2048]{1,0:T(2,128)(2,1)}) custom-call(bf16[2,2048]{1,0:T(2,128)(2,1)} %stream_in.1, bf16[3,2,2048]{2,1,0:T(2,128)(2,1)} %aqkv_in.1, bf16[3,128,2048]{2,1,0:T(8,128)(2,1)} %vqkv.1, bf16[128,2048]{1,0:T(8,128)(2,1)} %wo.1, f32[16,128]{1,0:T(8,128)} %bitcast.1, bf16[2048,512]{1,0:T(8,128)(2,1)} %w1.1, ...), custom_call_target="tpu_custom_call" | custom-call | tf_op jit(solution)/shard_map/cross_modal_layer/pallas_call | solution.py:360
  31.6 1.9 %write_results.1 = (bf16[128,2048]{1,0:T(8,128)(2,1)}, bf16[2,2048]{1,0:T(2,128)(2,1)}) custom-call(bf16[128,2048]{1,0:T(8,128)(2,1)} %get-tuple-element.4.mixed, bf16[2,2048]{1,0:T(2,128)(2,1)} %get-tuple-element.5.result), custom_call_target="tpu_custom_call" | custom-call | tf_op jit(solution)/shard_map/write_results/pallas_call | solution.py:414

commit v9 on v8

--- a/solution.py
+++ b/solution.py
@@ -237,8 +237,14 @@
         copy.start()
     p_recv[chip] = p_send[chip]
 
-    store = pltpu.make_async_copy(vmix, vmix_out, out_sem)
     v_group, v_window, v_windows, v_subs = windows_of(audio)
+    cuts = (0, v_windows // 4, 5 * v_windows // 8, v_windows)
+    stores = []
+    for i, (start, stop) in enumerate(((cuts[0], cuts[2]), (cuts[2], cuts[3]))):
+        span = pl.ds(start * v_window, (stop - start) * v_window)
+        stores.append(
+            pltpu.make_async_copy(vmix.at[:, span], vmix_out.at[:, span], out_sem.at[i])
+        )
 
     def video(start, stop):
         for w in range(start, stop):
@@ -285,7 +291,7 @@
     loads[3].wait()
     kmat[...] = rows_of(g_kv[:, 0:block])
     vmat[...] = rows_of(g_kv[:, block : 2 * block])
-    video(0, v_windows // 2)
+    video(cuts[0], cuts[1])
     all_of(a_recv, 3).wait_recv()
     mixed_audio = own + gathered_sum(a_recv)
 
@@ -294,8 +300,8 @@
     normed = by_token * lax.rsqrt(square / width + EPSILON) * gain[...][None]
     g_n[chip] = normed.reshape(block, LANES).astype(BF16)
     each_chip(lambda other, peer: remote(g_n.at[chip], g_n.at[chip], 4, peer).start())
-    video(v_windows // 2, v_windows)
-    store.start()
+    video(cuts[1], cuts[2])
+    stores[0].start()
     loads[7].wait()
     loads[8].wait()
     shared[3].wait_recv()
@@ -309,6 +315,8 @@
         term = mm(hidden, w2_v[k], 1, 0)
         part = term if part is None else part + term
     scatter(part, o_send, o_recv, 5)
+    video(cuts[2], cuts[3])
+    stores[1].start()
     all_of(o_recv, 5).wait_recv()
     relay_own[...] = mixed_audio + gathered_sum(o_recv)
     for c in range(chunks):
@@ -322,7 +330,8 @@
     all_of(g_kv, 6, far * (near - 1)).wait_send()
     for phase, ref in ((0, g_q), (2, p_send), (3, a_send), (4, g_n), (5, o_send)):
         all_of(ref, phase).wait_send()
-    store.wait()
+    for store in stores:
+        store.wait()
 
 
 def write_results(mixed, result, mixed_out, result_out, mixed_v, result_v, sem):
@@ -394,7 +403,7 @@
             by_chip,
             by_chip,
             pltpu.SemaphoreType.DMA((9,)),
-            pltpu.SemaphoreType.DMA,
+            pltpu.SemaphoreType.DMA((2,)),
             pltpu.SemaphoreType.DMA((12,)),
             pltpu.SemaphoreType.DMA((12,)),
         ],

time: 33.7 us -> 33.7 us (level)
  no operation moved by 1% of the time
where the time goes in v9:
time: 33.7 us; the launch traced here: 33.5 us
  Pallas kernels  32.9 us (98%)
  between operations  0.64 us (2%)
    pallas_call x1, Pallas kernels, local(): pl.pallas_call(functools.partial(kernel, n, math.gcd(n, NEAR)), out_shape...  31 us
    pallas_call x1, Pallas kernels, local(): pl.pallas_call(write_results, out_shape=(jax.ShapeDtypeStruct(mixed.shape...  1.85 us

profile of v9, /device:TPU:0, one launch (start us, length us, event | category | flops | bytes accessed | tf_op | source)
XLA Modules:
  0.0 33.5 jit_solution(11019402241074816569)
XLA Ops:
  0.6 31.0 %cross_modal_layer.1 = (bf16[128,2048]{1,0:T(8,128)(2,1)}, bf16[2,2048]{1,0:T(2,128)(2,1)}) custom-call(bf16[2,2048]{1,0:T(2,128)(2,1)} %stream_in.1, bf16[3,2,2048]{2,1,0:T(2,128)(2,1)} %aqkv_in.1, bf16[3,128,2048]{2,1,0:T(8,128)(2,1)} %vqkv.1, bf16[128,2048]{1,0:T(8,128)(2,1)} %wo.1, f32[16,128]{1,0:T(8,128)} %bitcast.1, bf16[2048,512]{1,0:T(8,128)(2,1)} %w1.1, ...), custom_call_target="tpu_custom_call" | custom-call | tf_op jit(solution)/shard_map/cross_modal_layer/pallas_call | solution.py:369
  31.6 1.9 %write_results.1 = (bf16[128,2048]{1,0:T(8,128)(2,1)}, bf16[2,2048]{1,0:T(2,128)(2,1)}) custom-call(bf16[128,2048]{1,0:T(8,128)(2,1)} %get-tuple-element.4.mixed, bf16[2,2048]{1,0:T(2,128)(2,1)} %get-tuple-element.5.result), custom_call_target="tpu_custom_call" | custom-call | tf_op jit(solution)/shard_map/write_results/pallas_call | solution.py:423
